TPU v7x, 512 devices: a whole 4x8x8 slice. The times are simulated.
512 devices in a mesh: seq: 64 (over y_hi, z, x), head: 8 (over y_lo, core).
Axes of the slice: x: 4, y: 8 (y_hi: 2, y_lo: 4; y = y_hi * 4 + y_lo), z: 8, core: 2. Of those that a mesh axis runs over, the one named last changes fastest.
Arguments:
- fw_query: bfloat16 [24576, 4096], P('seq', 'head'), may hold values from -6 to 6
- fw_key: bfloat16 [24576, 4096], P('seq', 'head'), may hold values from -6 to 6
- fw_value: bfloat16 [24576, 4096], P('seq', 'head'), may hold values from -6 to 6
- learn_rate: float32 [24576, 8], P('seq', 'head'), may hold values from 0.00012757759 to 0.001275776
- fast_weights: bfloat16 [3, 8, 512, 512], P(None, 'head'), may hold values from -0.25 to 0.25
- attn_query: bfloat16 [24576, 4096], P(('seq', 'head')), may hold values from -32 to 32
- attn_key: bfloat16 [24576, 1024], P(('seq', 'head')), may hold values from -32 to 32
- attn_value: bfloat16 [24576, 1024], P(('seq', 'head')), may hold values from -6 to 6
Outputs:
- mixed: bfloat16 [24576, 4096], P(('seq', 'head'))
All inputs are finite; a program needn't handle non-finite values.
Results may differ from a plain program's by a relative error of at most 0.01.
Values may be sent and summed in bfloat16 or wider, within the bound.
No kernel may reach another device: no remote copies, remote signals or barrier semaphores. Data moves between devices by JAX's collectives and lax.ppermute only.
A program may use at most 64 MiB of HBM per device.

v0:
```python
import math

import jax
import jax.numpy as jnp
from jax import lax
from jax.sharding import PartitionSpec as P

Q_HEADS = 32
KV_HEADS = 8
HEAD_DIM = 128
WINDOW = 256


def shifted(value, axis, by):
    devices = lax.axis_size(axis)
    pairs = [(i, i + by) for i in range(devices) if 0 <= i + by < devices]
    return lax.ppermute(value, axis, pairs)


def local_grads(keys, values, rates, weights):
    pre_gate = jnp.einsum("thd,hde->the", keys, weights[0], preferred_element_type=jnp.float32)
    pre_up = jnp.einsum("thd,hde->the", keys, weights[1], preferred_element_type=jnp.float32)
    sigm = jax.nn.sigmoid(pre_gate)
    hidden = (pre_gate * sigm * pre_up).astype(jnp.bfloat16)
    scaled = (rates[:, :, None] * values.astype(jnp.float32)).astype(jnp.bfloat16)
    back = jnp.einsum("the,hde->thd", scaled, weights[2], preferred_element_type=jnp.float32)
    d_gate = (back * pre_up * sigm * (1.0 + pre_gate * (1.0 - sigm))).astype(jnp.bfloat16)
    d_up = (back * pre_gate * sigm).astype(jnp.bfloat16)
    grad_gate = jnp.einsum("thd,the->hde", keys, d_gate, preferred_element_type=jnp.float32)
    grad_up = jnp.einsum("thd,the->hde", keys, d_up, preferred_element_type=jnp.float32)
    grad_down = jnp.einsum("thd,the->hde", hidden, scaled, preferred_element_type=jnp.float32)
    return jnp.stack([grad_gate, grad_up, grad_down])


def renorm(summed, start_weights):
    start = start_weights.astype(jnp.float32)
    stepped = start + summed
    ratio = jnp.sqrt(jnp.mean(start * start, axis=-2, keepdims=True)) * lax.rsqrt(
        jnp.mean(stepped * stepped, axis=-2, keepdims=True) + 1e-06
    )
    return (stepped * ratio).astype(jnp.bfloat16)


def on_device(
    fw_query, fw_key, fw_value, learn_rate, fast_weights, attn_query, attn_key, attn_value
):
    tok_rows = fw_key.shape[0]
    local_heads = fast_weights.shape[1]
    width = fast_weights.shape[2]
    keys = fw_key.reshape(tok_rows, local_heads, width)
    values = fw_value.reshape(tok_rows, local_heads, width)
    queries = fw_query.reshape(tok_rows, local_heads, width)
    grads = local_grads(keys, values, learn_rate, fast_weights)
    summed = lax.psum(grads, "seq")
    fresh = renorm(summed, fast_weights)
    q_gate = jnp.einsum("thd,hde->the", queries, fresh[0], preferred_element_type=jnp.float32)
    q_up = jnp.einsum("thd,hde->the", queries, fresh[1], preferred_element_type=jnp.float32)
    answer_hidden = (q_gate * jax.nn.sigmoid(q_gate) * q_up).astype(jnp.bfloat16)
    fw_out = jnp.einsum(
        "the,hef->thf", answer_hidden, fresh[2], preferred_element_type=jnp.float32
    ).astype(jnp.bfloat16)
    fw_out = fw_out.reshape(tok_rows, local_heads * width)
    fw_fine = lax.all_to_all(fw_out, "head", split_axis=0, concat_axis=1, tiled=True)
    rows = attn_query.shape[0]
    reach = -(-WINDOW // rows)
    kv_width = attn_key.shape[1]
    group = Q_HEADS // KV_HEADS
    buffer_k = jnp.zeros(((reach + 1) * rows, kv_width), jnp.bfloat16)
    buffer_v = jnp.zeros(((reach + 1) * rows, kv_width), jnp.bfloat16)
    buffer_k = lax.dynamic_update_slice_in_dim(buffer_k, attn_key, reach * rows, 0)
    buffer_v = lax.dynamic_update_slice_in_dim(buffer_v, attn_value, reach * rows, 0)

    def bring(step, carry):
        piece_k, piece_v, store_k, store_v = carry
        piece_k, piece_v = shifted((piece_k, piece_v), ("seq", "head"), 1)
        slot = (reach - 1 - step) * rows
        store_k = lax.dynamic_update_slice_in_dim(store_k, piece_k, slot, 0)
        store_v = lax.dynamic_update_slice_in_dim(store_v, piece_v, slot, 0)
        return (piece_k, piece_v, store_k, store_v)

    carried = lax.fori_loop(0, reach, bring, (attn_key, attn_value, buffer_k, buffer_v))
    buffer_k = carried[2].reshape((reach + 1) * rows, KV_HEADS, HEAD_DIM)
    buffer_v = carried[3].reshape((reach + 1) * rows, KV_HEADS, HEAD_DIM)
    device_pos = lax.axis_index("seq") * lax.axis_size("head") + lax.axis_index("head")
    t_pos = device_pos * rows + jnp.arange(rows, dtype=jnp.int32)
    s_pos = (device_pos - reach) * rows + jnp.arange((reach + 1) * rows, dtype=jnp.int32)
    gap = t_pos[:, None] - s_pos[None, :]
    keep = (gap >= 0) & (gap < WINDOW) & (s_pos[None, :] >= 0)
    query_heads = attn_query.reshape(rows, KV_HEADS, group, HEAD_DIM)
    scaling = 1.0 / math.sqrt(HEAD_DIM)
    scores = (
        jnp.einsum("fcgd,lcd->cgfl", query_heads, buffer_k, preferred_element_type=jnp.float32)
        * scaling
    )
    scores = jnp.where(keep, scores, -1e30)
    top = jnp.max(scores, axis=-1, keepdims=True)
    expo = jnp.exp(scores - top)
    probs = (expo / jnp.sum(expo, axis=-1, keepdims=True)).astype(jnp.bfloat16)
    attn_out = jnp.einsum("cgfl,lcd->fcgd", probs, buffer_v, preferred_element_type=jnp.float32)
    attn_out = attn_out.reshape(rows, Q_HEADS * HEAD_DIM)
    return (attn_out + fw_fine.astype(jnp.float32)).astype(jnp.bfloat16)


def solution(mesh):
    placed = (
        P("seq", "head"),
        P("seq", "head"),
        P("seq", "head"),
        P("seq", "head"),
        P(None, "head", None, None),
        P(("seq", "head"), None),
        P(("seq", "head"), None),
        P(("seq", "head"), None),
    )
    return jax.shard_map(
        on_device, mesh=mesh, in_specs=placed, out_specs=P(("seq", "head"), None), check_vma=False
    )
```

profile of v0, /device:TPU:57, one launch (start us, length us, event | category | flops | bytes accessed | tf_op | source)
XLA Modules:
  0.0 903.7 jit_solution(570671414931931289)
XLA Ops:
  6.5 1.7 copy.86
  8.2 1.5 copy.87
  9.8 1.4 convolution_bitcast_fusion.3
  11.2 0.4 convolution_bitcast_fusion.4
  11.6 1.4 convolution_bitcast_fusion.7
  13.0 1.6 convolution_bitcast_fusion
  14.6 0.6 convolution_bitcast_fusion.2
  15.2 0.5 convolution_bitcast_fusion.1
  15.7 2.0 pad_maximum_fusion
  17.8 0.7 copy.23
  18.5 1.0 dynamic_update_slice.20
  19.5 1.0 dynamic_update_slice.21
  20.4 69.0 %while.19 = (s32[]{:T(128)}, bf16[48,1024]{1,0:T(8,128)(2,1)}, bf16[48,1024]{1,0:T(8,128)(2,1)}, bf16[336,1024]{1,0:T(8,128)(2,1)S(1)}, bf16[336,1024]{1,0:T(8,1...) while((s32[]{:T(128)}, bf16[48,1024]{1,0:T(8,128)(2,1)}, ...), condition=%wide.region_1.0_spmd, body=%wide.region_0.0_spmd.sunk | while | flops 7 | bytes 1573111 | solution.py:81
  20.5 6.0 collective-permute-start
  26.5 1.9 collective-permute-start.1
  28.5 0.6 copy.79
  29.1 1.3 collective-permute-done.1
  30.4 0.6 copy.80
  31.1 6.9 collective-permute-start
  38.0 1.9 collective-permute-start.1
  39.9 0.6 copy.79
  40.6 1.3 collective-permute-done.1
  41.8 0.6 copy.80
  42.5 6.9 collective-permute-start
  49.4 1.9 collective-permute-start.1
  51.4 0.4 collective-permute-done
  51.8 0.6 copy.79
  52.4 0.9 collective-permute-done.1
  53.3 0.6 copy.80
  54.0 7.1 collective-permute-start
  61.1 1.9 collective-permute-start.1
  63.0 0.1 collective-permute-done
  63.1 0.6 copy.79
  63.7 1.6 collective-permute-done.1
  65.4 0.6 copy.80
  66.1 7.0 collective-permute-start
  73.1 1.9 collective-permute-start.1
  75.0 0.4 collective-permute-done
  75.5 0.6 copy.79
  76.1 1.0 collective-permute-done.1
  77.1 0.6 copy.80
  77.7 6.9 collective-permute-start
  84.7 1.9 collective-permute-start.1
  86.6 0.6 copy.79
  87.3 1.4 collective-permute-done.1
  88.7 0.6 copy.80
  89.4 1.0 copy.43
  90.4 2.0 reshape.133
  92.4 1.0 copy.42
  93.4 0.7 fusion.35
  94.1 735.5 %all-reduce.4.cloned.1.call-done = f32[3,1,512,512]{2,3,1,0:T(8,128)} async-done(((f32[3,1,512,512]{2,3,1,0:T(8,128)}), f32[3,1,512,512]{2,3,1,0:T(8,128)}) %all-reduce.4.cloned.1.call-update) | async-done | bytes 3145744 | tf_op jit(solution)/shard_map/psum | solution.py:54
  829.6 2.7 fusion.1
  832.5 0.4 multiply_convert_fusion
  832.9 0.6 copy-done.5
  833.5 0.4 convolution_bitcast_fusion.6
  833.9 2.5 convolution_convert_fusion
  836.4 49.6 %all-to-all-start = ((bf16[8,48,512]{2,1,0:T(8,128)(2,1)}), bf16[8,48,512]{2,1,0:T(8,128)(2,1)S(1)}, u32[]{:S(2)}, u32[]{:S(2)}) async-start(bf16[8,48,512]{2,1,0:T(8,128)(2,1)} %bitcast.109), calls=%async_computation | async-start | bytes 786432 | tf_op jit(solution)/shard_map/all_to_all | solution.py:63
  886.0 3.5 fusion.46
  889.6 2.2 convolution_bitcast_fusion.8
  891.8 0.3 copy.22
  892.1 0.3 reshape.134
  892.4 3.5 all-to-all-done
  895.9 0.1 convert_bitcast_fusion
  896.1 0.8 add_convert_fusion
  (38 shorter events, 0.4 us)
Async XLA Ops:
  6.5 3.2 copy-start
  6.5 5.0 copy-start.7
  6.5 4.6 copy-start.2
  6.5 823.1 %all-reduce.4.cloned.1.call-start = ((), (), s32[]{:S(2)}) async-start(), calls=%async_computation.1 | async-start | bytes 6291456 | tf_op jit(solution)/shard_map/psum | solution.py:54
  20.5 8.0 collective-permute-start
  26.5 3.9 collective-permute-start.1
  31.1 8.8 collective-permute-start
  38.0 3.9 collective-permute-start.1
  42.5 9.3 %collective-permute-start = (bf16[48,1024]{1,0:T(8,128)(2,1)}, bf16[48,1024]{1,0:T(8,128)(2,1)S(1)}, u32[]{:S(2)}, u32[]{:S(2)}) collective-permute-start(bf16[48,1024]{1,0:T(8,128)(2,1)} %get-tuple-element.158), channel_id=1, source_target_pairs={{0,1},{1,2},{2,3},{3,4},{4,5},{5,6},{6,7},{7,8},{8,9},{9,10},{10,1... | collective-permute-start | bytes 294920 | tf_op jit(solution)/shard_map/while/body/eval_jaxpr/ppermute | solution.py:17
  49.4 3.9 collective-permute-start.1
  54.0 9.1 %collective-permute-start = (bf16[48,1024]{1,0:T(8,128)(2,1)}, bf16[48,1024]{1,0:T(8,128)(2,1)S(1)}, u32[]{:S(2)}, u32[]{:S(2)}) collective-permute-start(bf16[48,1024]{1,0:T(8,128)(2,1)} %get-tuple-element.158), channel_id=1, source_target_pairs={{0,1},{1,2},{2,3},{3,4},{4,5},{5,6},{6,7},{7,8},{8,9},{9,10},{10,1... | collective-permute-start | bytes 294920 | tf_op jit(solution)/shard_map/while/body/eval_jaxpr/ppermute | solution.py:17
  61.1 4.3 collective-permute-start.1
  66.1 9.4 %collective-permute-start = (bf16[48,1024]{1,0:T(8,128)(2,1)}, bf16[48,1024]{1,0:T(8,128)(2,1)S(1)}, u32[]{:S(2)}, u32[]{:S(2)}) collective-permute-start(bf16[48,1024]{1,0:T(8,128)(2,1)} %get-tuple-element.158), channel_id=1, source_target_pairs={{0,1},{1,2},{2,3},{3,4},{4,5},{5,6},{6,7},{7,8},{8,9},{9,10},{10,1... | collective-permute-start | bytes 294920 | tf_op jit(solution)/shard_map/while/body/eval_jaxpr/ppermute | solution.py:17
  73.1 3.9 collective-permute-start.1
  77.7 8.9 collective-permute-start
  84.7 4.0 collective-permute-start.1
  829.6 2.8 copy-start.1
  832.5 1.0 copy-start.5
  833.9 52.2 %copy-start.4 = (bf16[42,8,8,128]{3,2,1,0:T(8,128)(2,1)S(1)}, bf16[42,8,8,128]{3,2,1,0:T(8,128)(2,1)}, u32[]{:S(2)}) copy-start(bf16[42,8,8,128]{3,2,1,0:T(8,128)(2,1)} %copy.43) | copy-start | bytes 2064388
  833.9 52.2 %copy-start.6 = (pred[48,336]{1,0:T(8,128)(4,1)S(1)}, pred[48,336]{1,0:T(8,128)(4,1)}, u32[]{:S(2)}) copy-start(pred[48,336]{1,0:T(8,128)(4,1)} %fusion.35) | copy-start | bytes 48388
  836.4 59.5 %all-to-all-start = ((bf16[8,48,512]{2,1,0:T(8,128)(2,1)}), bf16[8,48,512]{2,1,0:T(8,128)(2,1)S(1)}, u32[]{:S(2)}, u32[]{:S(2)}) async-start(bf16[8,48,512]{2,1,0:T(8,128)(2,1)} %bitcast.109), calls=%async_computation | async-start | bytes 786432 | tf_op jit(solution)/shard_map/all_to_all | solution.py:63
  886.0 3.5 copy-start.3
Sparse Core Ops, SparseCore 0:
  17.9 811.6 all-reduce.3
where the time goes:
time: 908 us; the launch traced here: 904 us
  waiting for transfers between devices  747 us (82%)
  starting transfers between devices  102 us (11%)
  local copies, waits for them, and re-layouts  19 us (2%)
  matrix products  14.5 us (2%)
  between operations  13.6 us (1%)
    psum x1, waiting for transfers between devices, on_device(): summed = lax.psum(grads, 'seq')  735 us
    ppermute x12, starting transfers between devices, shifted(): return lax.ppermute(value, axis, pairs)  52.4 us
    all_to_all x1, starting transfers between devices, on_device(): lax.all_to_all(fw_out, 'head', split_axis=0, concat_axis=1, tiled=True)  49.6 us
  transfers between devices with their start and end apart: 14, of which 11 were waited for; matrix products, arithmetic and copies ran while one was open for 2% of the time, Pallas kernels for 0%

commit v1 on v0

v1 whole, which is shorter than its diff:
```python
import math

import jax
import jax.numpy as jnp
from jax import lax
from jax.sharding import Mesh, PartitionSpec as P

Q_HEADS = 32
KV_HEADS = 8
HEAD_DIM = 128
WINDOW = 256

FINE = (("yh", 2), ("zh", 4), ("zl", 2), ("x", 4), ("yl", 4), ("core", 2))
SEQ = ("yh", "zh", "zl", "x")
HEAD = ("yl", "core")
INNER = ("x",)
OUTER = ("yh", "zh", "zl")


def shifted(value, by):
    axes = SEQ + HEAD
    devices = lax.axis_size(axes)
    return lax.ppermute(value, axes, [(i, i + by) for i in range(devices - by)])


def spread(value, axes):
    devices = lax.axis_size(axes)
    many = jnp.broadcast_to(value[None], (devices,) + value.shape)
    return lax.all_to_all(many, axes, 0, 0, tiled=True)


def local_grads(keys, values, rates, weights):
    pre_gate = jnp.dot(keys, weights[0], preferred_element_type=jnp.float32)
    pre_up = jnp.dot(keys, weights[1], preferred_element_type=jnp.float32)
    sigm = jax.nn.sigmoid(pre_gate)
    hidden = (pre_gate * sigm * pre_up).astype(jnp.bfloat16)
    scaled = (rates * values.astype(jnp.float32)).astype(jnp.bfloat16)
    back = jnp.einsum("te,de->td", scaled, weights[2], preferred_element_type=jnp.float32)
    d_gate = (back * pre_up * sigm * (1.0 + pre_gate * (1.0 - sigm))).astype(jnp.bfloat16)
    d_up = (back * pre_gate * sigm).astype(jnp.bfloat16)

    def product(left, right):
        return jnp.einsum("te,td->ed", left, right, preferred_element_type=jnp.float32)

    return product(d_gate, keys), product(d_up, keys), product(scaled, hidden)


def on_device(
    fw_query, fw_key, fw_value, learn_rate, fast_weights, attn_query, attn_key, attn_value
):
    rows = attn_query.shape[0]
    kv = jnp.concatenate([attn_key, attn_value], axis=1)
    one = shifted(kv, 1)
    two = shifted(jnp.concatenate([one, kv]), 2)
    three = shifted(jnp.concatenate([two[rows:], one, kv]), 4)
    near = jnp.concatenate([three, two, one, kv])

    weights = fast_weights[:, 0]
    width = weights.shape[1]
    inner, outer = lax.axis_size(INNER), lax.axis_size(OUTER)
    part = width // (inner * outer)
    grads = local_grads(fw_key, fw_value, learn_rate, weights)
    pieces = jnp.stack(
        [g.astype(jnp.bfloat16).reshape(inner, outer, part, width) for g in grads], axis=2
    )
    pieces = lax.all_to_all(pieces, INNER, 0, 0, tiled=True)
    pieces = jnp.sum(pieces.astype(jnp.float32), axis=0).astype(jnp.bfloat16)
    pieces = lax.all_to_all(pieces, OUTER, 0, 0, tiled=True)
    summed = jnp.sum(pieces.astype(jnp.float32), axis=0)

    mine = (lax.axis_index(INNER) * outer + lax.axis_index(OUTER)) * part
    start = lax.dynamic_slice_in_dim(weights, mine, part, 2).transpose(0, 2, 1)
    start = start.astype(jnp.float32)
    stepped = start + summed
    ratio = jnp.sqrt(jnp.mean(start * start, axis=-1, keepdims=True)) * lax.rsqrt(
        jnp.mean(stepped * stepped, axis=-1, keepdims=True) + 1e-06
    )
    fresh = (stepped * ratio).astype(jnp.bfloat16)
    fresh = spread(spread(fresh, OUTER), INNER)
    fresh = fresh.reshape(inner * outer, 3, part, width)
    new_gate, new_up, new_down = (fresh[:, m].reshape(width, width) for m in range(3))

    def product(left, right):
        return jnp.einsum("td,ed->te", left, right, preferred_element_type=jnp.float32)

    q_gate = product(fw_query, new_gate)
    q_up = product(fw_query, new_up)
    answer_hidden = (q_gate * jax.nn.sigmoid(q_gate) * q_up).astype(jnp.bfloat16)
    fw_out = product(answer_hidden, new_down).astype(jnp.bfloat16)
    fw_fine = lax.all_to_all(fw_out.reshape(-1, rows, width), HEAD, 0, 0, tiled=True)
    fw_fine = fw_fine.transpose(1, 0, 2).reshape(rows, -1)

    span = near.shape[0]
    near_k, near_v = (near[:, i * 1024 : (i + 1) * 1024] for i in range(2))
    near_k = near_k.reshape(span, KV_HEADS, HEAD_DIM)
    near_v = near_v.reshape(span, KV_HEADS, HEAD_DIM)
    group = Q_HEADS // KV_HEADS
    t_pos = lax.axis_index(SEQ + HEAD) * rows + jnp.arange(rows, dtype=jnp.int32)
    s_pos = lax.axis_index(SEQ + HEAD) * rows + rows - span + jnp.arange(span, dtype=jnp.int32)
    gap = t_pos[:, None] - s_pos[None, :]
    keep = (gap >= 0) & (gap < WINDOW) & (s_pos[None, :] >= 0)
    query_heads = attn_query.reshape(rows, KV_HEADS, group, HEAD_DIM)
    scaling = 1.0 / math.sqrt(HEAD_DIM)
    scores = (
        jnp.einsum("fcgd,lcd->cgfl", query_heads, near_k, preferred_element_type=jnp.float32)
        * scaling
    )
    scores = jnp.where(keep, scores, -1e30)
    top = jnp.max(scores, axis=-1, keepdims=True)
    expo = jnp.exp(scores - top)
    probs = (expo / jnp.sum(expo, axis=-1, keepdims=True)).astype(jnp.bfloat16)
    attn_out = jnp.einsum("cgfl,lcd->fcgd", probs, near_v, preferred_element_type=jnp.float32)
    attn_out = attn_out.reshape(rows, Q_HEADS * HEAD_DIM)
    return (attn_out + fw_fine.astype(jnp.float32)).astype(jnp.bfloat16)


def solution(mesh):
    fine = Mesh(
        mesh.devices.reshape([size for _, size in FINE]), tuple(name for name, _ in FINE)
    )
    placed = (
        P(SEQ, HEAD),
        P(SEQ, HEAD),
        P(SEQ, HEAD),
        P(SEQ, HEAD),
        P(None, HEAD, None, None),
        P(SEQ + HEAD, None),
        P(SEQ + HEAD, None),
        P(SEQ + HEAD, None),
    )
    return jax.shard_map(
        on_device, mesh=fine, in_specs=placed, out_specs=P(SEQ + HEAD, None), check_vma=False
    )
```

time: 908 us -> 160 us (0.18)
  waiting for transfers between devices: 747 us -> 40 us
  starting transfers between devices: 102 us -> 66.8 us
  blocking collectives: 0 us -> 23.6 us
  between operations: 13.6 us -> 0.33 us
  local copies, waits for them, and re-layouts: 19 us -> 9.18 us
    psum x1 -> x0, waiting for transfers between devices: 735 us -> none  [on_device(): summed = lax.psum(grads, 'seq')]
    ppermute x12 -> x3, starting transfers between devices: 52.4 us -> 21.4 us  [shifted(): return lax.ppermute(value, axes, [(i, i + by) for i in range(devices - by)])]
    ppermute x12 -> x3, waiting for transfers between devices: 8.37 us -> 34.3 us  [shifted(): return lax.ppermute(value, axes, [(i, i + by) for i in range(devices - by)])]
    all_to_all x0 -> x1, blocking collectives: none -> 23.6 us  [on_device(): pieces = lax.all_to_all(pieces, INNER, 0, 0, tiled=True)]
    all_to_all x1 -> x4, starting transfers between devices: 49.6 us -> 45.4 us  [the longest x2 15.6 us: spread(): return lax.all_to_all(many, axes, 0, 0, tiled=True)]
  transfers between devices with their start and end apart: 14 -> 7, of which waited for: 11 -> 4; matrix products, arithmetic and copies ran while one was open for 2% -> 8% of each run, Pallas kernels for 0% -> 0%
where the time goes in v1:
time: 160 us; the launch traced here: 159 us
  starting transfers between devices  66.8 us (42%)
  waiting for transfers between devices  40 us (25%)
  blocking collectives  23.6 us (15%)
  matrix products  14.6 us (9%)
  local copies, waits for them, and re-layouts  9.18 us (6%)
  other arithmetic  4.38 us (3%)
    ppermute x3, waiting for transfers between devices, shifted(): return lax.ppermute(value, axes, [(i, i + by) for i in range(devices - by)])  34.3 us
    all_to_all x1, blocking collectives, on_device(): pieces = lax.all_to_all(pieces, INNER, 0, 0, tiled=True)  23.6 us
    ppermute x3, starting transfers between devices, shifted(): return lax.ppermute(value, axes, [(i, i + by) for i in range(devices - by)])  21.4 us
    all_to_all x2, starting transfers between devices, spread(): return lax.all_to_all(many, axes, 0, 0, tiled=True)  15.6 us
    all_to_all x1, starting transfers between devices, on_device(): pieces = lax.all_to_all(pieces, OUTER, 0, 0, tiled=True)  15.1 us
    all_to_all x1, starting transfers between devices, on_device(): lax.all_to_all(fw_out.reshape(-1, rows, width), HEAD, 0, 0, tiled=True)  14.6 us
    dot_general x2, matrix products, product(): jnp.einsum('td,ed->te', left, right, preferred_element_type=jnp.float32)  3.84 us
    sub x1, matrix products, on_device(): expo = jnp.exp(scores - top)  3.51 us
  transfers between devices with their start and end apart: 7, of which 4 were waited for; matrix products, arithmetic and copies ran while one was open for 8% of the time, Pallas kernels for 0%

profile of v1, /device:TPU:57, one launch (start us, length us, event | category | flops | bytes accessed | tf_op | source)
XLA Modules:
  0.0 158.9 jit_solution(7257383707388531264)
XLA Ops:
  0.0 0.0 copy-start
  0.0 0.0 copy-start.1
  0.0 0.0 copy-start.9
  0.0 1.0 copy-done
  1.0 1.4 fusion.17
  2.4 0.0 copy-done.1
  2.4 0.4 fusion.15
  2.8 0.0 copy-done.9
  2.8 0.0 copy-start.5
  2.8 1.5 fusion.19
  4.3 0.0 copy-done.5
  4.3 0.6 convolution_convert_fusion
  4.9 0.5 convolution_convert_fusion.1
  5.5 0.6 convolution_convert_fusion.2
  6.1 0.2 pad_maximum_fusion
  6.3 23.6 %all_to_all.25 = bf16[4,16,3,8,512]{4,3,1,2,0:T(8,128)(2,1)S(1)} all-to-all(bf16[4,16,3,8,512]{4,3,1,2,0:T(8,128)(2,1)S(1)} %pad_maximum_fusion), channel_id=1, replica_groups=mesh['yh'=2,'zh'=4,'zl'=2,'x'=4,'yl'=4,'core'=2] {'x'}, dimensions={0} | all-to-all | bytes 3145728 | tf_op jit(solution)/shard_map/all_to_all | solution.py:66
  29.9 1.1 reduce_sum.49
  31.0 0.0 copy-start.6
  31.0 0.0 copy-start.7
  31.0 1.8 %copy.41 = bf16[16,3,8,512]{3,2,1,0:T(8,128)(2,1)} copy(bf16[16,3,8,512]{3,2,0,1:T(8,128)(2,1)} %reduce_sum.49) | data formatting | bytes 786432 | tf_op jit(solution)/shard_map/reduce_sum | solution.py:67
  32.8 15.1 %all-to-all-start.1 = ((bf16[16,3,8,512]{3,2,1,0:T(8,128)(2,1)}), bf16[16,3,8,512]{3,2,1,0:T(8,128)(2,1)S(1)}, u32[]{:S(2)}, u32[]{:S(2)}) async-start(bf16[16,3,8,512]{3,2,1,0:T(8,128)(2,1)} %copy.41), calls=%async_computation.1 | async-start | bytes 786432 | tf_op jit(solution)/shard_map/all_to_all | solution.py:68
  47.9 0.0 copy-done.6
  48.0 0.0 copy-done.7
  48.0 0.0 copy-start.2
  48.0 6.9 %collective-permute-start = (bf16[48,2048]{1,0:T(8,128)(2,1)S(1)}, bf16[48,2048]{1,0:T(8,128)(2,1)S(1)}, u32[]{:S(2)}, u32[]{:S(2)}) collective-permute-start(bf16[48,2048]{1,0:T(8,128)(2,1)S(1)} %constant_dynamic-update-slice_fusion), channel_id=1, source_target_pairs={{0,1},{1,2},{2,3},{3,4},{4,5},{5,6},{6,7},{7,8},{8,9},{9,10},{10,1... | collective-permute-start | bytes 589832 | tf_op jit(solution)/shard_map/ppermute | solution.py:23
  54.9 0.2 constant_dynamic-slice_fusion
  55.1 0.1 copy.56
  55.2 2.2 %all-to-all-done.1 = bf16[16,3,8,512]{3,2,1,0:T(8,128)(2,1)S(1)} async-done(((bf16[16,3,8,512]{3,2,1,0:T(8,128)(2,1)}), bf16[16,3,8,512]{3,2,1,0:T(8,128)(2,1)S(1)}, u32[]{:S(2)}, u32[]{:S(2)}) %all-to-all-start.1) | async-done | bytes 393248 | tf_op jit(solution)/shard_map/all_to_all | solution.py:68
  57.4 0.1 convert_reduce_fusion
  57.5 0.1 fusion.38
  57.6 0.1 multiply_convert_fusion.9
  57.7 0.8 broadcast_in_dim.12
  58.4 12.0 %all-to-all-start.2 = ((bf16[16,3,8,512]{3,2,1,0:T(8,128)(2,1)}), bf16[16,3,8,512]{3,2,1,0:T(8,128)(2,1)S(1)}, u32[]{:S(2)}, u32[]{:S(2)}) async-start(bf16[16,3,8,512]{3,2,1,0:T(8,128)(2,1)} %broadcast_in_dim.12), calls=%async_computation.2 | async-start | bytes 786432 | tf_op jit(solution)/shard_map/all_to_all | solution.py:29
  70.4 0.0 collective-permute-done
  70.4 0.0 copy-done.2
  70.4 4.5 %collective-permute-start.1 = (bf16[96,2048]{1,0:T(8,128)(2,1)S(1)}, bf16[96,2048]{1,0:T(8,128)(2,1)S(1)}, u32[]{:S(2)}, u32[]{:S(2)}) collective-permute-start(bf16[96,2048]{1,0:T(8,128)(2,1)S(1)} %pad_maximum_fusion.3), channel_id=1, source_target_pairs={{0,2},{1,3},{2,4},{3,5},{4,6},{5,7},{6,8},{7,9},{8,10},{9,11},{10,... | collective-permute-start | bytes 1179656 | tf_op jit(solution)/shard_map/ppermute | solution.py:23
  75.0 12.0 %collective-permute-done.1 = bf16[96,2048]{1,0:T(8,128)(2,1)S(1)} collective-permute-done((bf16[96,2048]{1,0:T(8,128)(2,1)S(1)}, bf16[96,2048]{1,0:T(8,128)(2,1)S(1)}, u32[]{:S(2)}, u32[]{:S(2)}) %collective-permute-start.1) | collective-permute-done | bytes 393248 | tf_op jit(solution)/shard_map/ppermute | solution.py:23
  87.0 0.0 all-to-all-done.2
  87.0 1.3 broadcast_in_dim.13
  88.3 3.7 %all-to-all-start.3 = ((bf16[4,16,3,8,512]{4,3,2,1,0:T(8,128)(2,1)}), bf16[4,16,3,8,512]{4,3,2,1,0:T(8,128)(2,1)S(1)}, u32[]{:S(2)}, u32[]{:S(2)}) async-start(bf16[4,16,3,8,512]{4,3,2,1,0:T(8,128)(2,1)} %broadcast_in_dim.13), calls=%async_computation.3 | async-start | bytes 3145728 | tf_op jit(solution)/shard_map/all_to_all | solution.py:29
  92.0 0.0 copy-done.3
  92.1 10.1 %collective-permute-start.2 = (bf16[144,2048]{1,0:T(8,128)(2,1)S(1)}, bf16[144,2048]{1,0:T(8,128)(2,1)}, u32[]{:S(2)}, u32[]{:S(2)}) collective-permute-start(bf16[144,2048]{1,0:T(8,128)(2,1)S(1)} %pad_maximum_fusion.2), channel_id=1, source_target_pairs={{0,4},{1,5},{2,6},{3,7},{4,8},{5,9},{6,10},{7,11},{8,12},{9,13},{1... | collective-permute-start | bytes 1769480 | tf_op jit(solution)/shard_map/ppermute | solution.py:23
  102.2 2.0 %reshape.64 = bf16[48,8,4,128]{3,2,1,0:T(4,128)(2,1)} reshape(bf16[48,4096]{1,0:T(8,128)(2,1)} %param.13) | data formatting | bytes 786432 | tf_op jit(solution)/shard_map/reshape | solution.py:102
  104.2 0.7 fusion.35
  104.9 22.3 %collective-permute-done.2 = bf16[144,2048]{1,0:T(8,128)(2,1)} collective-permute-done((bf16[144,2048]{1,0:T(8,128)(2,1)S(1)}, bf16[144,2048]{1,0:T(8,128)(2,1)}, u32[]{:S(2)}, u32[]{:S(2)}) %collective-permute-start.2) | collective-permute-done | bytes 589856 | tf_op jit(solution)/shard_map/ppermute | solution.py:23
  127.2 1.2 pad_maximum_fusion.1
  128.4 0.1 slice_bitcast_fusion.1
  128.5 0.1 copy.59
  128.6 1.0 copy.58
  129.6 0.0 all-to-all-done.3
  129.6 1.4 convolution_bitcast_fusion.1
  131.0 0.0 copy-start.8
  131.0 2.5 %convolution_convert_fusion.3 = bf16[384,512]{1,0:T(8,128)(2,1)} fusion(bf16[384,512]{1,0:T(8,128)(2,1)} %param.8, f32[384,512]{1,0:T(8,128)S(1)} %convolution_bitcast_fusion.1, bf16[64,3,8,512]{3,2,1,0:T(8,128)(2,1)S(1)} %bitcast.88), kind=kOutput, calls=%fused_computation.15 | convolution fusion | flops 404029440 | bytes 2621440 | tf_op jit(solution)/shard_map/td,ed->te/dot_general | solution.py:84
  133.5 14.6 %all-to-all-start.4 = ((bf16[8,48,512]{2,1,0:T(8,128)(2,1)}), bf16[8,48,512]{2,1,0:T(8,128)(2,1)S(1)}, u32[]{:S(2)}, u32[]{:S(2)}) async-start(bf16[8,48,512]{2,1,0:T(8,128)(2,1)} %bitcast.94), calls=%async_computation.4 | async-start | bytes 786432 | tf_op jit(solution)/shard_map/all_to_all | solution.py:90
  148.1 0.0 copy-done.8
  148.1 3.5 %fusion.49 = (f32[8,4,48]{2,1,0:T(4,128)S(1)}, f32[8,4,48,336]{3,2,1,0:T(8,128)}) fusion(pred[48,336]{1,0:T(8,128)(4,1)S(1)} %copy-done.8, bf16[48,8,4,128]{3,2,1,0:T(4,128)(2,1)} %reshape.64, bf16[336,8,128,1]{2,1,0,3:T(8,128)(2,1)S(1)} %bitcast.89), kind=kOutput, calls=%fused_computation.76 | convolution fusion | flops 134185296 | bytes 3168000 | tf_op jit(solution)/shard_map/sub | solution.py:110
  151.6 0.0 copy-done.4
  151.6 2.2 %convolution_bitcast_fusion.2 = f32[48,8,4,128]{3,0,2,1:T(8,128)S(1)} fusion(f32[8,4,48,336]{3,2,1,0:T(8,128)} %get-tuple-element.10, f32[8,4,48]{2,1,0:T(4,128)S(1)} %get-tuple-element.9, bf16[336,8,128,1]{2,1,0,3:T(8,128)(2,1)S(1)} %bitcast.90), kind=kOutput, calls=%fused_computation.13 | convolution fusion | flops 133152768 | bytes 3545088 | tf_op jit(solution)/shard_map/cgfl,lcd->fcgd/dot_general | solution.py:112
  153.8 0.3 copy.35
  154.1 0.3 reshape.65
  154.5 3.5 %all-to-all-done.4 = bf16[8,48,512]{2,1,0:T(8,128)(2,1)S(1)} async-done(((bf16[8,48,512]{2,1,0:T(8,128)(2,1)}), bf16[8,48,512]{2,1,0:T(8,128)(2,1)S(1)}, u32[]{:S(2)}, u32[]{:S(2)}) %all-to-all-start.4) | async-done | bytes 393248 | tf_op jit(solution)/shard_map/all_to_all | solution.py:90
  158.0 0.1 convert_bitcast_fusion
  158.0 0.1 copy.57
  158.1 0.8 add_convert_fusion
  (12 shorter events, 0.2 us)
Async XLA Ops:
  0.0 1.0 copy-start
  0.0 2.4 %copy-start.1 = (bf16[3,1,512,512]{3,2,1,0:T(8,128)(2,1)S(1)}, bf16[3,1,512,512]{3,2,1,0:T(8,128)(2,1)}, u32[]{:S(2)}) copy-start(bf16[3,1,512,512]{3,2,1,0:T(8,128)(2,1)} %param.12) | copy-start | bytes 4718596
  0.0 2.8 %copy-start.9 = (f32[384,1]{0,1:T(1,128)S(1)}, f32[384,1]{0,1:T(1,128)}, u32[]{:S(2)}) copy-start(f32[384,1]{0,1:T(1,128)} %param.11) | copy-start | bytes 4612
  2.8 1.5 copy-start.5
  31.0 17.0 %copy-start.6 = (bf16[48,1024]{1,0:T(8,128)(2,1)S(1)}, bf16[48,1024]{1,0:T(8,128)(2,1)}, u32[]{:S(2)}) copy-start(bf16[48,1024]{1,0:T(8,128)(2,1)} %param.14) | copy-start | bytes 294916
  31.0 17.0 %copy-start.7 = (bf16[48,1024]{1,0:T(8,128)(2,1)S(1)}, bf16[48,1024]{1,0:T(8,128)(2,1)}, u32[]{:S(2)}) copy-start(bf16[48,1024]{1,0:T(8,128)(2,1)} %param.15) | copy-start | bytes 294916
  32.8 24.6 %all-to-all-start.1 = ((bf16[16,3,8,512]{3,2,1,0:T(8,128)(2,1)}), bf16[16,3,8,512]{3,2,1,0:T(8,128)(2,1)S(1)}, u32[]{:S(2)}, u32[]{:S(2)}) async-start(bf16[16,3,8,512]{3,2,1,0:T(8,128)(2,1)} %copy.41), calls=%async_computation.1 | async-start | bytes 786432 | tf_op jit(solution)/shard_map/all_to_all | solution.py:68
  48.0 22.5 %copy-start.2 = (bf16[48,2048]{1,0:T(8,128)(2,1)}, bf16[48,2048]{1,0:T(8,128)(2,1)S(1)}, u32[]{:S(2)}) copy-start(bf16[48,2048]{1,0:T(8,128)(2,1)S(1)} %constant_dynamic-update-slice_fusion) | copy-start | bytes 589828
  48.0 22.4 %collective-permute-start = (bf16[48,2048]{1,0:T(8,128)(2,1)S(1)}, bf16[48,2048]{1,0:T(8,128)(2,1)S(1)}, u32[]{:S(2)}, u32[]{:S(2)}) collective-permute-start(bf16[48,2048]{1,0:T(8,128)(2,1)S(1)} %constant_dynamic-update-slice_fusion), channel_id=1, source_target_pairs={{0,1},{1,2},{2,3},{3,4},{4,5},{5,6},{6,7},{7,8},{8,9},{9,10},{10,1... | collective-permute-start | bytes 589832 | tf_op jit(solution)/shard_map/ppermute | solution.py:23
  58.4 28.6 %all-to-all-start.2 = ((bf16[16,3,8,512]{3,2,1,0:T(8,128)(2,1)}), bf16[16,3,8,512]{3,2,1,0:T(8,128)(2,1)S(1)}, u32[]{:S(2)}, u32[]{:S(2)}) async-start(bf16[16,3,8,512]{3,2,1,0:T(8,128)(2,1)} %broadcast_in_dim.12), calls=%async_computation.2 | async-start | bytes 786432 | tf_op jit(solution)/shard_map/all_to_all | solution.py:29
  70.4 16.6 %collective-permute-start.1 = (bf16[96,2048]{1,0:T(8,128)(2,1)S(1)}, bf16[96,2048]{1,0:T(8,128)(2,1)S(1)}, u32[]{:S(2)}, u32[]{:S(2)}) collective-permute-start(bf16[96,2048]{1,0:T(8,128)(2,1)S(1)} %pad_maximum_fusion.3), channel_id=1, source_target_pairs={{0,2},{1,3},{2,4},{3,5},{4,6},{5,7},{6,8},{7,9},{8,10},{9,11},{10,... | collective-permute-start | bytes 1179656 | tf_op jit(solution)/shard_map/ppermute | solution.py:23
  88.3 3.7 %copy-start.3 = (bf16[48,2048]{1,0:T(8,128)(2,1)S(1)}, bf16[48,2048]{1,0:T(8,128)(2,1)}, u32[]{:S(2)}) copy-start(bf16[48,2048]{1,0:T(8,128)(2,1)} %copy-done.2) | copy-start | bytes 589828
  88.3 41.3 %all-to-all-start.3 = ((bf16[4,16,3,8,512]{4,3,2,1,0:T(8,128)(2,1)}), bf16[4,16,3,8,512]{4,3,2,1,0:T(8,128)(2,1)S(1)}, u32[]{:S(2)}, u32[]{:S(2)}) async-start(bf16[4,16,3,8,512]{4,3,2,1,0:T(8,128)(2,1)} %broadcast_in_dim.13), calls=%async_computation.3 | async-start | bytes 3145728 | tf_op jit(solution)/shard_map/all_to_all | solution.py:29
  92.1 35.1 %collective-permute-start.2 = (bf16[144,2048]{1,0:T(8,128)(2,1)S(1)}, bf16[144,2048]{1,0:T(8,128)(2,1)}, u32[]{:S(2)}, u32[]{:S(2)}) collective-permute-start(bf16[144,2048]{1,0:T(8,128)(2,1)S(1)} %pad_maximum_fusion.2), channel_id=1, source_target_pairs={{0,4},{1,5},{2,6},{3,7},{4,8},{5,9},{6,10},{7,11},{8,12},{9,13},{1... | collective-permute-start | bytes 1769480 | tf_op jit(solution)/shard_map/ppermute | solution.py:23
  131.0 17.1 %copy-start.8 = (pred[48,336]{1,0:T(8,128)(4,1)S(1)}, pred[48,336]{1,0:T(8,128)(4,1)}, u32[]{:S(2)}) copy-start(pred[48,336]{1,0:T(8,128)(4,1)} %fusion.35) | copy-start | bytes 48388
  133.5 24.5 %all-to-all-start.4 = ((bf16[8,48,512]{2,1,0:T(8,128)(2,1)}), bf16[8,48,512]{2,1,0:T(8,128)(2,1)S(1)}, u32[]{:S(2)}, u32[]{:S(2)}) async-start(bf16[8,48,512]{2,1,0:T(8,128)(2,1)} %bitcast.94), calls=%async_computation.4 | async-start | bytes 786432 | tf_op jit(solution)/shard_map/all_to_all | solution.py:90
  148.1 3.5 %copy-start.4 = (bf16[42,8,8,128]{3,2,1,0:T(8,128)(2,1)S(1)}, bf16[42,8,8,128]{3,2,1,0:T(8,128)(2,1)}, u32[]{:S(2)}) copy-start(bf16[42,8,8,128]{3,2,1,0:T(8,128)(2,1)} %copy.58) | copy-start | bytes 2064388

commit v2 on v1

v2 whole, which is shorter than its diff:
```python
import functools
import math

import jax
import jax.numpy as jnp
from jax import lax
from jax.experimental import pallas as pl
from jax.experimental.pallas import tpu as pltpu
from jax.sharding import Mesh, PartitionSpec as P

Q_HEADS = 32
KV_HEADS = 8
HEAD_DIM = 128
WINDOW = 256
MIB = 1 << 20

FINE = (("yh", 2), ("zh", 4), ("zl", 2), ("xh", 2), ("xl", 2), ("yl", 4), ("core", 2))
SEQ = ("yh", "zh", "zl", "xh", "xl")
HEAD = ("yl", "core")
NEAR = ("zl", "xl")
FAR = ("zh", "xh")

F32 = jnp.float32
BF16 = jnp.bfloat16
ROWS_ROWS = (((0,), (0,)), ((), ()))
COLS_COLS = (((1,), (1,)), ((), ()))


def next_chip(value):
    axes = SEQ + HEAD
    devices = lax.axis_size(axes)
    return lax.ppermute(value, axes, [(i, i + 2) for i in range(devices - 2)])


def swapped(value, axis):
    return lax.ppermute(value, axis, [(0, 1), (1, 0)])


def after(value, first):
    return lax.optimization_barrier((value, first))


def call(body, out, args, mib, flops=0):
    moved = sum(a.size * a.dtype.itemsize for a in args) + out.size * out.dtype.itemsize
    return pl.pallas_call(
        body,
        out_shape=out,
        compiler_params=pltpu.CompilerParams(vmem_limit_bytes=mib * MIB),
        cost_estimate=pl.CostEstimate(flops=flops, bytes_accessed=moved, transcendentals=0),
    )(*args)


def dot(left, right, dims=(((1,), (0,)), ((), ()))):
    return lax.dot_general(left, right, dims, preferred_element_type=F32)


def grads_body(k_ref, v_ref, rate_ref, w_ref, out_ref):
    close, far, _, part, width = out_ref.shape
    block = width // 2
    keys = k_ref[...]
    rates = rate_ref[...].reshape(keys.shape[0], 1)
    scaled = (rates * v_ref[...].astype(F32)).astype(BF16)
    for start in range(0, width, block):
        cols = slice(start, start + block)
        gate = dot(keys, w_ref[0, :, cols])
        up = dot(keys, w_ref[1, :, cols])
        back = dot(scaled, w_ref[2, cols, :], COLS_COLS)
        sigm = jax.nn.sigmoid(gate)
        act = gate * sigm
        hidden = (act * up).astype(BF16)
        d_gate = (back * up * sigm * (1.0 + gate * (1.0 - sigm))).astype(BF16)
        d_up = (back * act).astype(BF16)
        half = slice(start * close // width, (start + block) * close // width)
        shape = (close * block // width, far, part, width)
        out_ref[half, :, 0] = dot(d_gate, keys, ROWS_ROWS).astype(BF16).reshape(shape)
        out_ref[half, :, 1] = dot(d_up, keys, ROWS_ROWS).astype(BF16).reshape(shape)
        down = dot(scaled, hidden, ROWS_ROWS).astype(BF16)
        out_ref[:, :, 2, :, cols] = down.reshape(close, far, part, block)


def sum_body(in_ref, out_ref):
    total = in_ref[0].astype(F32)
    for i in range(1, in_ref.shape[0]):
        total = total + in_ref[i].astype(F32)
    out_ref[...] = total.astype(out_ref.dtype)


def renorm_body(half_ref, other_ref, start_ref, out_ref):
    start = start_ref[...].astype(F32)
    stepped = start + (half_ref[...] + other_ref[...])
    ratio = jnp.sqrt(jnp.mean(start * start, axis=-1, keepdims=True)) * lax.rsqrt(
        jnp.mean(stepped * stepped, axis=-1, keepdims=True) + 1e-06
    )
    fresh = (stepped * ratio).astype(BF16)
    for i in range(out_ref.shape[0]):
        out_ref[i] = fresh


def copies_body(in_ref, out_ref):
    for i in range(out_ref.shape[0]):
        out_ref[i] = in_ref[...]


def answer_body(q_ref, w_ref, out_ref):
    width = q_ref.shape[1]
    query = q_ref[...]
    gate_w, up_w, down_w = (w_ref[:, :, m].reshape(width, width) for m in range(3))
    gate = dot(query, gate_w, COLS_COLS)
    up = dot(query, up_w, COLS_COLS)
    hidden = (gate * jax.nn.sigmoid(gate) * up).astype(BF16)
    out_ref[...] = dot(hidden, down_w, COLS_COLS).astype(BF16).reshape(out_ref.shape)


def attend_body(place_ref, q_ref, *refs):
    *kv_refs, swap_ref, out_ref = refs
    rows = q_ref.shape[0]
    links = len(kv_refs)
    span = 2 * links * rows
    group = Q_HEADS // KV_HEADS
    kv_width = KV_HEADS * HEAD_DIM
    device, other = place_ref[0], place_ref[1]
    key = lax.broadcasted_iota(jnp.int32, (1, span), 1)
    s_pos = key + device * rows
    for i in range(1, 2 * links):
        origin = device - 2 * i if i < links else other - 2 * (i - links)
        s_pos = jnp.where(key >= i * rows, key + (origin - i) * rows, s_pos)
    t_pos = device * rows + lax.broadcasted_iota(jnp.int32, (rows, 1), 0)
    gap = t_pos - s_pos
    keep = (gap >= 0) & (gap < WINDOW) & (s_pos >= 0)
    keep = jnp.concatenate([keep] * group, axis=0)
    scaling = 1.0 / math.sqrt(HEAD_DIM)
    for c in range(KV_HEADS):
        own = slice(c * HEAD_DIM, (c + 1) * HEAD_DIM)
        vals = slice(kv_width + c * HEAD_DIM, kv_width + (c + 1) * HEAD_DIM)
        keys = jnp.concatenate([r[:, own] for r in kv_refs] + [swap_ref[:, own]], axis=0)
        values = jnp.concatenate([r[:, vals] for r in kv_refs] + [swap_ref[:, vals]], axis=0)
        heads = [slice((c * group + j) * HEAD_DIM, (c * group + j + 1) * HEAD_DIM) for j in range(group)]
        query = jnp.concatenate([q_ref[:, h] for h in heads], axis=0)
        scores = jnp.where(keep, dot(query, keys, COLS_COLS) * scaling, -1e30)
        expo = jnp.exp(scores - jnp.max(scores, axis=-1, keepdims=True))
        probs = (expo / jnp.sum(expo, axis=-1, keepdims=True)).astype(BF16)
        result = dot(probs, values)
        for j, h in enumerate(heads):
            out_ref[:, h] = result[j * rows : (j + 1) * rows]


def mix_body(attn_ref, fw_ref, out_ref):
    width = fw_ref.shape[2]
    for h in range(fw_ref.shape[0]):
        cols = slice(h * width, (h + 1) * width)
        out_ref[:, cols] = (attn_ref[:, cols] + fw_ref[h].astype(F32)).astype(BF16)


def on_device(
    fw_query, fw_key, fw_value, learn_rate, fast_weights, attn_query, attn_key, attn_value
):
    rows = attn_query.shape[0]
    tok_rows, width = fw_key.shape
    weights = fast_weights[:, 0]
    close, far = lax.axis_size(NEAR), lax.axis_size(FAR)
    part = width // (close * far)
    shape = jax.ShapeDtypeStruct
    product = 2 * tok_rows * width * width

    kv = [jnp.concatenate([attn_key, attn_value], axis=1)]
    pieces = call(
        grads_body,
        shape((close, far, 3, part, width), BF16),
        (fw_key, fw_value, learn_rate.reshape(1, tok_rows), weights),
        32,
        6 * product,
    )
    pieces = lax.all_to_all(pieces, NEAR, 0, 0, tiled=True)
    kv.append(next_chip(kv[-1]))
    pieces, kv[-1] = after(pieces, kv[-1])
    pieces = call(sum_body, shape((far, 3, part, width), BF16), (pieces,), 16)
    pieces = lax.all_to_all(pieces, FAR, 0, 0, tiled=True)
    half = call(sum_body, shape((3, part, width), F32), (pieces,), 16)
    kv.append(next_chip(kv[-1]))
    half, kv[-1] = after(half, kv[-1])

    mine = (lax.axis_index(NEAR) * far + lax.axis_index(FAR)) * part
    start = lax.dynamic_slice_in_dim(weights, mine, part, 2).transpose(0, 2, 1)
    other = swapped(half, "yh")
    fresh = call(renorm_body, shape((far, 3, part, width), BF16), (half, other, start), 16)
    fresh = lax.all_to_all(fresh, FAR, 0, 0, tiled=True)
    kv.append(next_chip(kv[-1]))
    fresh, kv[-1] = after(fresh, kv[-1])
    fresh = call(copies_body, shape((close, far, 3, part, width), BF16), (fresh,), 16)
    fresh = lax.all_to_all(fresh, NEAR, 0, 0, tiled=True)
    swap = swapped(jnp.concatenate(kv), "core")

    fw_out = call(
        answer_body,
        shape((tok_rows // rows, rows, width), BF16),
        (fw_query, fresh),
        24,
        3 * product,
    )
    fw_fine = lax.all_to_all(fw_out, HEAD, 0, 0, tiled=True)
    device = lax.axis_index(SEQ + HEAD)
    place = jnp.stack([device, device + 1 - 2 * lax.axis_index("core")])
    attn = pl.pallas_call(
        attend_body,
        out_shape=shape(attn_query.shape, F32),
        in_specs=[pl.BlockSpec(memory_space=pltpu.SMEM)]
        + [pl.BlockSpec(memory_space=pltpu.VMEM)] * (len(kv) + 2),
        compiler_params=pltpu.CompilerParams(vmem_limit_bytes=24 * MIB),
        cost_estimate=pl.CostEstimate(flops=10**9, bytes_accessed=3 * MIB, transcendentals=0),
    )(place, attn_query, *kv, swap)
    return call(mix_body, shape(attn_query.shape, BF16), (attn, fw_fine), 16)


def solution(mesh):
    fine = Mesh(
        mesh.devices.reshape([size for _, size in FINE]), tuple(name for name, _ in FINE)
    )
    placed = (
        P(SEQ, HEAD),
        P(SEQ, HEAD),
        P(SEQ, HEAD),
        P(SEQ, HEAD),
        P(None, HEAD, None, None),
        P(SEQ + HEAD, None),
        P(SEQ + HEAD, None),
        P(SEQ + HEAD, None),
    )
    return jax.shard_map(
        on_device, mesh=fine, in_specs=placed, out_specs=P(SEQ + HEAD, None), check_vma=False
    )
```

time: 160 us -> 139 us (0.87)
  the two profiles are of different devices: /device:TPU:57 before, /device:TPU:1 now
where the time goes in v2:
time: 139 us; the launch traced here: 138 us
  starting transfers between devices  62 us (45%)
  waiting for transfers between devices  55.5 us (40%)
  Pallas kernels  12.7 us (9%)
  local copies, waits for them, and re-layouts  6.42 us (5%)
    ppermute x2, starting transfers between devices, swapped(): return lax.ppermute(value, axis, [(0, 1), (1, 0)])  15.1 us
    all_to_all x1, waiting for transfers between devices, on_device(): pieces = lax.all_to_all(pieces, NEAR, 0, 0, tiled=True)  14.7 us
    all_to_all x1, waiting for transfers between devices, on_device(): fresh = lax.all_to_all(fresh, NEAR, 0, 0, tiled=True)  13.8 us
    all_to_all x1, starting transfers between devices, on_device(): pieces = lax.all_to_all(pieces, FAR, 0, 0, tiled=True)  12.4 us
    all_to_all x1, starting transfers between devices, on_device(): fresh = lax.all_to_all(fresh, NEAR, 0, 0, tiled=True)  10.4 us
    pallas_call x7, Pallas kernels, call(): pl.pallas_call(body, out_shape=out, compiler_params=pltpu.CompilerParams(...  9.12 us
    all_to_all x1, waiting for transfers between devices, on_device(): pieces = lax.all_to_all(pieces, FAR, 0, 0, tiled=True)  8.36 us
    all_to_all x1, starting transfers between devices, on_device(): fresh = lax.all_to_all(fresh, FAR, 0, 0, tiled=True)  7.1 us
  transfers between devices with their start and end apart: 10, of which 8 were waited for; matrix products, arithmetic and copies ran while one was open for 2% of the time, Pallas kernels for 4%

profile of v2, /device:TPU:1, one launch (start us, length us, event | category | flops | bytes accessed | tf_op | source)
XLA Modules:
  0.0 137.7 jit_solution(13336763482332022005)
XLA Ops:
  0.0 0.0 copy-start.1
  0.0 1.4 %copy-done.1 = bf16[3,1,512,512]{3,2,1,0:T(8,128)(2,1)S(1)} copy-done((bf16[3,1,512,512]{3,2,1,0:T(8,128)(2,1)S(1)}, bf16[3,1,512,512]{3,2,1,0:T(8,128)(2,1)}, u32[]{:S(2)}) %copy-start.1) | copy-done | bytes 1572888
  1.4 0.0 copy-start.2
  1.4 1.0 copy-done.2
  2.4 0.0 copy-start.3
  2.4 1.0 copy-done.3
  3.4 0.0 copy-start.5
  3.4 0.7 copy-done.5
  4.1 3.6 %shard_map.82 = bf16[4,8,3,16,512]{4,3,2,1,0:T(8,128)(2,1)} custom-call(bf16[384,512]{1,0:T(8,128)(2,1)S(1)} %copy-done.2, bf16[384,512]{1,0:T(8,128)(2,1)S(1)} %copy-done.3, f32[1,384]{1,0:T(1,128)S(1)} %bitcast.9, bf16[3,512,512]{2,1,0:T(8,128)(2,1)S(1)} %bitcast.8), custom_call_target="tpu_custom_call" | custom-call | flops 1207959552 | bytes 3933696 | tf_op jit(solution)/shard_map/pallas_call | solution.py:45
  7.7 0.0 copy-start.6
  7.7 0.0 copy-start.7
  7.7 5.3 %all-to-all-start = ((bf16[4,8,3,16,512]{4,3,2,1,0:T(8,128)(2,1)}), bf16[4,8,3,16,512]{4,3,2,1,0:T(8,128)(2,1)S(1)}, u32[]{:S(2)}, u32[]{:S(2)}) async-start(bf16[4,8,3,16,512]{4,3,2,1,0:T(8,128)(2,1)} %shard_map.82), calls=%async_computation | async-start | bytes 3145728 | tf_op jit(solution)/shard_map/all_to_all | solution.py:173
  12.9 0.0 copy-done.6
  12.9 0.0 copy-done.7
  13.0 3.2 %collective-permute-start = (bf16[48,2048]{1,0:T(8,128)(2,1)S(1)}, bf16[48,2048]{1,0:T(8,128)(2,1)S(1)}, u32[]{:S(2)}, u32[]{:S(2)}) collective-permute-start(bf16[48,2048]{1,0:T(8,128)(2,1)S(1)} %constant_dynamic-update-slice_fusion.refs_0_), channel_id=1, source_target_pairs={{0,2},{1,3},{2,4},{3,5},{4,6},{5,7},{6,8},{7,9},{8,10},{9,11},{10,... | collective-permute-start | bytes 589832 | tf_op jit(solution)/shard_map/ppermute | solution.py:32
  16.2 2.6 %collective-permute-done.refs_1_ = bf16[48,2048]{1,0:T(8,128)(2,1)S(1)} collective-permute-done((bf16[48,2048]{1,0:T(8,128)(2,1)S(1)}, bf16[48,2048]{1,0:T(8,128)(2,1)S(1)}, u32[]{:S(2)}, u32[]{:S(2)}) %collective-permute-start) | collective-permute-done | bytes 196640 | tf_op jit(solution)/shard_map/ppermute | solution.py:32
  18.8 14.7 %all-to-all-done.in_ref = bf16[4,8,3,16,512]{4,3,2,1,0:T(8,128)(2,1)S(1)} async-done(((bf16[4,8,3,16,512]{4,3,2,1,0:T(8,128)(2,1)}), bf16[4,8,3,16,512]{4,3,2,1,0:T(8,128)(2,1)S(1)}, u32[]{:S(2)}, u32[]{:S(2)}) %all-to-all-start) | async-done | bytes 1572896 | tf_op jit(solution)/shard_map/all_to_all | solution.py:173
  33.5 0.9 shard_map.83
  34.4 12.4 %all-to-all-start.1 = ((bf16[8,3,16,512]{3,2,1,0:T(8,128)(2,1)}), bf16[8,3,16,512]{3,2,1,0:T(8,128)(2,1)S(1)}, u32[]{:S(2)}, u32[]{:S(2)}) async-start(bf16[8,3,16,512]{3,2,1,0:T(8,128)(2,1)} %shard_map.83), calls=%async_computation.1 | async-start | bytes 786432 | tf_op jit(solution)/shard_map/all_to_all | solution.py:177
  46.8 1.3 collective-permute-start.1
  48.1 8.4 %all-to-all-done.1.in_ref = bf16[8,3,16,512]{3,2,1,0:T(8,128)(2,1)S(1)} async-done(((bf16[8,3,16,512]{3,2,1,0:T(8,128)(2,1)}), bf16[8,3,16,512]{3,2,1,0:T(8,128)(2,1)S(1)}, u32[]{:S(2)}, u32[]{:S(2)}) %all-to-all-start.1) | async-done | bytes 393248 | tf_op jit(solution)/shard_map/all_to_all | solution.py:177
  56.5 0.1 shard_map.84.half_ref
  56.5 0.0 collective-permute-done.1.refs_2_
  56.5 11.1 %collective-permute-start.2 = (f32[3,16,512]{2,1,0:T(8,128)S(1)}, f32[3,16,512]{2,1,0:T(8,128)S(1)}, u32[]{:S(2)}, u32[]{:S(2)}) collective-permute-start(f32[3,16,512]{2,1,0:T(8,128)S(1)} %shard_map.84.half_ref), channel_id=1, source_target_pairs={{0,256},{256,0},{1,257},{257,1},{2,258},{258,2},{3,259},{259,3},{4... | collective-permute-start | bytes 294920 | tf_op jit(solution)/shard_map/ppermute | solution.py:36
  67.7 1.2 constant_dynamic-slice_fusion
  68.9 0.1 copy.9
  69.0 0.8 collective-permute-done.2.other_ref
  69.8 0.9 shard_map.85
  70.6 7.1 %all-to-all-start.2 = ((bf16[8,3,16,512]{3,2,1,0:T(8,128)(2,1)}), bf16[8,3,16,512]{3,2,1,0:T(8,128)(2,1)S(1)}, u32[]{:S(2)}, u32[]{:S(2)}) async-start(bf16[8,3,16,512]{3,2,1,0:T(8,128)(2,1)} %shard_map.85), calls=%async_computation.2 | async-start | bytes 786432 | tf_op jit(solution)/shard_map/all_to_all | solution.py:186
  77.8 1.5 %collective-permute-start.3 = (bf16[48,2048]{1,0:T(8,128)(2,1)S(1)}, bf16[48,2048]{1,0:T(8,128)(2,1)S(1)}, u32[]{:S(2)}, u32[]{:S(2)}) collective-permute-start(bf16[48,2048]{1,0:T(8,128)(2,1)S(1)} %collective-permute-done.1.refs_2_), channel_id=1, source_target_pairs={{0,2},{1,3},{2,4},{3,5},{4,6},{5,7},{6,8},{7,9},{8,10},{9,11},{10,... | collective-permute-start | bytes 589832 | tf_op jit(solution)/shard_map/ppermute | solution.py:32
  79.3 2.6 %collective-permute-done.3.refs_3_ = bf16[48,2048]{1,0:T(8,128)(2,1)S(1)} collective-permute-done((bf16[48,2048]{1,0:T(8,128)(2,1)S(1)}, bf16[48,2048]{1,0:T(8,128)(2,1)S(1)}, u32[]{:S(2)}, u32[]{:S(2)}) %collective-permute-start.3) | collective-permute-done | bytes 196640 | tf_op jit(solution)/shard_map/ppermute | solution.py:32
  81.9 5.7 %all-to-all-done.2.in_ref = bf16[8,3,16,512]{3,2,1,0:T(8,128)(2,1)S(1)} async-done(((bf16[8,3,16,512]{3,2,1,0:T(8,128)(2,1)}), bf16[8,3,16,512]{3,2,1,0:T(8,128)(2,1)S(1)}, u32[]{:S(2)}, u32[]{:S(2)}) %all-to-all-start.2) | async-done | bytes 393248 | tf_op jit(solution)/shard_map/all_to_all | solution.py:186
  87.6 1.3 shard_map.87
  88.8 0.0 copy-start
  88.8 10.4 %all-to-all-start.3 = ((bf16[4,8,3,16,512]{4,3,2,1,0:T(8,128)(2,1)}), bf16[4,8,3,16,512]{4,3,2,1,0:T(8,128)(2,1)S(1)}, u32[]{:S(2)}, u32[]{:S(2)}) async-start(bf16[4,8,3,16,512]{4,3,2,1,0:T(8,128)(2,1)} %shard_map.87), calls=%async_computation.3 | async-start | bytes 3145728 | tf_op jit(solution)/shard_map/all_to_all | solution.py:190
  99.2 1.0 pad_maximum_fusion
  100.2 4.0 %collective-permute-start.4 = (bf16[192,2048]{1,0:T(8,128)(2,1)}, bf16[192,2048]{1,0:T(8,128)(2,1)S(1)}, u32[]{:S(2)}, u32[]{:S(2)}) collective-permute-start(bf16[192,2048]{1,0:T(8,128)(2,1)} %pad_maximum_fusion), channel_id=1, source_target_pairs={{0,1},{1,0},{2,3},{3,2},{4,5},{5,4},{6,7},{7,6},{8,9},{9,8},{10,11... | collective-permute-start | bytes 2359304 | tf_op jit(solution)/shard_map/ppermute | solution.py:36
  104.1 13.8 %all-to-all-done.3.w_ref = bf16[4,8,3,16,512]{4,3,2,1,0:T(8,128)(2,1)S(1)} async-done(((bf16[4,8,3,16,512]{4,3,2,1,0:T(8,128)(2,1)}), bf16[4,8,3,16,512]{4,3,2,1,0:T(8,128)(2,1)S(1)}, u32[]{:S(2)}, u32[]{:S(2)}) %all-to-all-start.3) | async-done | bytes 1572896 | tf_op jit(solution)/shard_map/all_to_all | solution.py:190
  117.9 0.0 copy-done
  117.9 1.6 %shard_map.88 = bf16[8,48,512]{2,1,0:T(8,128)(2,1)} custom-call(bf16[384,512]{1,0:T(8,128)(2,1)S(1)} %copy-done, bf16[4,8,3,16,512]{4,3,2,1,0:T(8,128)(2,1)S(1)} %all-to-all-done.3.w_ref), custom_call_target="tpu_custom_call" | custom-call | flops 603979776 | bytes 2359296 | tf_op jit(solution)/shard_map/pallas_call | solution.py:45
  119.5 5.7 %all-to-all-start.4 = ((bf16[8,48,512]{2,1,0:T(8,128)(2,1)}), bf16[8,48,512]{2,1,0:T(8,128)(2,1)S(1)}, u32[]{:S(2)}, u32[]{:S(2)}) async-start(bf16[8,48,512]{2,1,0:T(8,128)(2,1)} %shard_map.88), calls=%async_computation.4 | async-start | bytes 786432 | tf_op jit(solution)/shard_map/all_to_all | solution.py:200
  125.2 0.1 pad_add_fusion.place_ref
  125.3 0.0 collective-permute-done.4.refs_4_
  125.3 0.0 copy-start.4
  125.3 1.0 copy-done.4
  126.3 3.6 %shard_map.86.attn_ref = f32[48,4096]{1,0:T(8,128)S(1)} custom-call(s32[2]{0:T(128)S(1)} %pad_add_fusion.place_ref, bf16[48,4096]{1,0:T(8,128)(2,1)S(1)} %copy-done.4, bf16[48,2048]{1,0:T(8,128)(2,1)S(1)} %constant_dynamic-update-slice_fusion.refs_0_, bf16[48,2048]{1,0:T(8,128)(2,1)S(1)} %collective-permute-done.refs_1_, ...), custom_call_target="tpu_custom_call" | custom-call | flops 1000000000 | bytes 3145728 | tf_op jit(solution)/shard_map/pallas_call | solution.py:203
  129.9 7.0 %all-to-all-done.4.fw_ref = bf16[8,48,512]{2,1,0:T(8,128)(2,1)S(1)} async-done(((bf16[8,48,512]{2,1,0:T(8,128)(2,1)}), bf16[8,48,512]{2,1,0:T(8,128)(2,1)S(1)}, u32[]{:S(2)}, u32[]{:S(2)}) %all-to-all-start.4) | async-done | bytes 393248 | tf_op jit(solution)/shard_map/all_to_all | solution.py:200
  136.9 0.8 shard_map.89
  (2 shorter events, 0.0 us)
Async XLA Ops:
  0.0 1.4 %copy-start.1 = (bf16[3,1,512,512]{3,2,1,0:T(8,128)(2,1)S(1)}, bf16[3,1,512,512]{3,2,1,0:T(8,128)(2,1)}, u32[]{:S(2)}) copy-start(bf16[3,1,512,512]{3,2,1,0:T(8,128)(2,1)} %param.12) | copy-start | bytes 4718596
  1.4 1.0 copy-start.2
  2.4 1.0 copy-start.3
  3.4 0.7 copy-start.5
  7.7 5.3 %copy-start.6 = (bf16[48,1024]{1,0:T(8,128)(2,1)S(1)}, bf16[48,1024]{1,0:T(8,128)(2,1)}, u32[]{:S(2)}) copy-start(bf16[48,1024]{1,0:T(8,128)(2,1)} %param.14) | copy-start | bytes 294916
  7.7 5.3 %copy-start.7 = (bf16[48,1024]{1,0:T(8,128)(2,1)S(1)}, bf16[48,1024]{1,0:T(8,128)(2,1)}, u32[]{:S(2)}) copy-start(bf16[48,1024]{1,0:T(8,128)(2,1)} %param.15) | copy-start | bytes 294916
  7.7 25.8 %all-to-all-start = ((bf16[4,8,3,16,512]{4,3,2,1,0:T(8,128)(2,1)}), bf16[4,8,3,16,512]{4,3,2,1,0:T(8,128)(2,1)S(1)}, u32[]{:S(2)}, u32[]{:S(2)}) async-start(bf16[4,8,3,16,512]{4,3,2,1,0:T(8,128)(2,1)} %shard_map.82), calls=%async_computation | async-start | bytes 3145728 | tf_op jit(solution)/shard_map/all_to_all | solution.py:173
  13.0 5.8 %collective-permute-start = (bf16[48,2048]{1,0:T(8,128)(2,1)S(1)}, bf16[48,2048]{1,0:T(8,128)(2,1)S(1)}, u32[]{:S(2)}, u32[]{:S(2)}) collective-permute-start(bf16[48,2048]{1,0:T(8,128)(2,1)S(1)} %constant_dynamic-update-slice_fusion.refs_0_), channel_id=1, source_target_pairs={{0,2},{1,3},{2,4},{3,5},{4,6},{5,7},{6,8},{7,9},{8,10},{9,11},{10,... | collective-permute-start | bytes 589832 | tf_op jit(solution)/shard_map/ppermute | solution.py:32
  34.4 22.1 %all-to-all-start.1 = ((bf16[8,3,16,512]{3,2,1,0:T(8,128)(2,1)}), bf16[8,3,16,512]{3,2,1,0:T(8,128)(2,1)S(1)}, u32[]{:S(2)}, u32[]{:S(2)}) async-start(bf16[8,3,16,512]{3,2,1,0:T(8,128)(2,1)} %shard_map.83), calls=%async_computation.1 | async-start | bytes 786432 | tf_op jit(solution)/shard_map/all_to_all | solution.py:177
  46.8 9.7 %collective-permute-start.1 = (bf16[48,2048]{1,0:T(8,128)(2,1)S(1)}, bf16[48,2048]{1,0:T(8,128)(2,1)S(1)}, u32[]{:S(2)}, u32[]{:S(2)}) collective-permute-start(bf16[48,2048]{1,0:T(8,128)(2,1)S(1)} %collective-permute-done.refs_1_), channel_id=1, source_target_pairs={{0,2},{1,3},{2,4},{3,5},{4,6},{5,7},{6,8},{7,9},{8,10},{9,11},{10,... | collective-permute-start | bytes 589832 | tf_op jit(solution)/shard_map/ppermute | solution.py:32
  56.5 13.2 %collective-permute-start.2 = (f32[3,16,512]{2,1,0:T(8,128)S(1)}, f32[3,16,512]{2,1,0:T(8,128)S(1)}, u32[]{:S(2)}, u32[]{:S(2)}) collective-permute-start(f32[3,16,512]{2,1,0:T(8,128)S(1)} %shard_map.84.half_ref), channel_id=1, source_target_pairs={{0,256},{256,0},{1,257},{257,1},{2,258},{258,2},{3,259},{259,3},{4... | collective-permute-start | bytes 294920 | tf_op jit(solution)/shard_map/ppermute | solution.py:36
  70.6 16.9 %all-to-all-start.2 = ((bf16[8,3,16,512]{3,2,1,0:T(8,128)(2,1)}), bf16[8,3,16,512]{3,2,1,0:T(8,128)(2,1)S(1)}, u32[]{:S(2)}, u32[]{:S(2)}) async-start(bf16[8,3,16,512]{3,2,1,0:T(8,128)(2,1)} %shard_map.85), calls=%async_computation.2 | async-start | bytes 786432 | tf_op jit(solution)/shard_map/all_to_all | solution.py:186
  77.8 4.1 %collective-permute-start.3 = (bf16[48,2048]{1,0:T(8,128)(2,1)S(1)}, bf16[48,2048]{1,0:T(8,128)(2,1)S(1)}, u32[]{:S(2)}, u32[]{:S(2)}) collective-permute-start(bf16[48,2048]{1,0:T(8,128)(2,1)S(1)} %collective-permute-done.1.refs_2_), channel_id=1, source_target_pairs={{0,2},{1,3},{2,4},{3,5},{4,6},{5,7},{6,8},{7,9},{8,10},{9,11},{10,... | collective-permute-start | bytes 589832 | tf_op jit(solution)/shard_map/ppermute | solution.py:32
  88.8 29.1 %copy-start = (bf16[384,512]{1,0:T(8,128)(2,1)S(1)}, bf16[384,512]{1,0:T(8,128)(2,1)}, u32[]{:S(2)}) copy-start(bf16[384,512]{1,0:T(8,128)(2,1)} %q_ref.3) | copy-start | bytes 1179652
  88.8 29.1 %all-to-all-start.3 = ((bf16[4,8,3,16,512]{4,3,2,1,0:T(8,128)(2,1)}), bf16[4,8,3,16,512]{4,3,2,1,0:T(8,128)(2,1)S(1)}, u32[]{:S(2)}, u32[]{:S(2)}) async-start(bf16[4,8,3,16,512]{4,3,2,1,0:T(8,128)(2,1)} %shard_map.87), calls=%async_computation.3 | async-start | bytes 3145728 | tf_op jit(solution)/shard_map/all_to_all | solution.py:190
  100.2 25.1 %collective-permute-start.4 = (bf16[192,2048]{1,0:T(8,128)(2,1)}, bf16[192,2048]{1,0:T(8,128)(2,1)S(1)}, u32[]{:S(2)}, u32[]{:S(2)}) collective-permute-start(bf16[192,2048]{1,0:T(8,128)(2,1)} %pad_maximum_fusion), channel_id=1, source_target_pairs={{0,1},{1,0},{2,3},{3,2},{4,5},{5,4},{6,7},{7,6},{8,9},{9,8},{10,11... | collective-permute-start | bytes 2359304 | tf_op jit(solution)/shard_map/ppermute | solution.py:36
  119.5 17.4 %all-to-all-start.4 = ((bf16[8,48,512]{2,1,0:T(8,128)(2,1)}), bf16[8,48,512]{2,1,0:T(8,128)(2,1)S(1)}, u32[]{:S(2)}, u32[]{:S(2)}) async-start(bf16[8,48,512]{2,1,0:T(8,128)(2,1)} %shard_map.88), calls=%async_computation.4 | async-start | bytes 786432 | tf_op jit(solution)/shard_map/all_to_all | solution.py:200
  125.3 1.0 copy-start.4

commit v3 on v2

--- a/solution.py
+++ b/solution.py
@@ -14,11 +14,11 @@
 WINDOW = 256
 MIB = 1 << 20
 
-FINE = (("yh", 2), ("zh", 4), ("zl", 2), ("xh", 2), ("xl", 2), ("yl", 4), ("core", 2))
-SEQ = ("yh", "zh", "zl", "xh", "xl")
+FINE = (("yh", 2), ("zh", 4), ("zl", 2), ("x", 4), ("yl", 4), ("core", 2))
+SEQ = ("yh", "zh", "zl", "x")
 HEAD = ("yl", "core")
-NEAR = ("zl", "xl")
-FAR = ("zh", "xh")
+NEAR = ("zl", "x")
+FAR = ("zh",)
 
 F32 = jnp.float32
 BF16 = jnp.bfloat16
@@ -54,16 +54,37 @@
     return lax.dot_general(left, right, dims, preferred_element_type=F32)
 
 
-def grads_body(k_ref, v_ref, rate_ref, w_ref, out_ref):
+def grads_body(k_hbm, v_hbm, rate_ref, w_hbm, out_ref, k_ref, v_ref, w_ref, sems):
     close, far, _, part, width = out_ref.shape
     block = width // 2
+    copies = [
+        pltpu.make_async_copy(source, target, sems.at[i])
+        for i, (source, target) in enumerate(
+            (
+                (k_hbm, k_ref),
+                (w_hbm.at[0], w_ref.at[0]),
+                (w_hbm.at[1], w_ref.at[1]),
+                (v_hbm, v_ref),
+                (w_hbm.at[2], w_ref.at[2]),
+            )
+        )
+    ]
+    for copy in copies:
+        copy.start()
+    copies[0].wait()
+    copies[1].wait()
     keys = k_ref[...]
-    rates = rate_ref[...].reshape(keys.shape[0], 1)
-    scaled = (rates * v_ref[...].astype(F32)).astype(BF16)
     for start in range(0, width, block):
         cols = slice(start, start + block)
         gate = dot(keys, w_ref[0, :, cols])
+        if start == 0:
+            copies[2].wait()
         up = dot(keys, w_ref[1, :, cols])
+        if start == 0:
+            copies[3].wait()
+            rates = rate_ref[...].reshape(keys.shape[0], 1)
+            scaled = (rates * v_ref[...].astype(F32)).astype(BF16)
+            copies[4].wait()
         back = dot(scaled, w_ref[2, cols, :], COLS_COLS)
         sigm = jax.nn.sigmoid(gate)
         act = gate * sigm
@@ -163,25 +184,33 @@
     product = 2 * tok_rows * width * width
 
     kv = [jnp.concatenate([attn_key, attn_value], axis=1)]
-    pieces = call(
+    hbm = pl.BlockSpec(memory_space=pltpu.HBM)
+    vmem = pl.BlockSpec(memory_space=pltpu.VMEM)
+    pieces = pl.pallas_call(
         grads_body,
-        shape((close, far, 3, part, width), BF16),
-        (fw_key, fw_value, learn_rate.reshape(1, tok_rows), weights),
-        32,
-        6 * product,
-    )
+        out_shape=shape((close, far, 3, part, width), BF16),
+        in_specs=[hbm, hbm, vmem, hbm],
+        scratch_shapes=[
+            pltpu.VMEM((tok_rows, width), BF16),
+            pltpu.VMEM((tok_rows, width), BF16),
+            pltpu.VMEM((3, width, width), BF16),
+            pltpu.SemaphoreType.DMA((5,)),
+        ],
+        compiler_params=pltpu.CompilerParams(vmem_limit_bytes=60 * MIB),
+        cost_estimate=pl.CostEstimate(flops=6 * product, bytes_accessed=4 * MIB, transcendentals=0),
+    )(fw_key, fw_value, learn_rate.reshape(1, tok_rows), weights)
     pieces = lax.all_to_all(pieces, NEAR, 0, 0, tiled=True)
     kv.append(next_chip(kv[-1]))
     pieces, kv[-1] = after(pieces, kv[-1])
     pieces = call(sum_body, shape((far, 3, part, width), BF16), (pieces,), 16)
     pieces = lax.all_to_all(pieces, FAR, 0, 0, tiled=True)
     half = call(sum_body, shape((3, part, width), F32), (pieces,), 16)
-    kv.append(next_chip(kv[-1]))
-    half, kv[-1] = after(half, kv[-1])
 
     mine = (lax.axis_index(NEAR) * far + lax.axis_index(FAR)) * part
     start = lax.dynamic_slice_in_dim(weights, mine, part, 2).transpose(0, 2, 1)
     other = swapped(half, "yh")
+    kv.append(next_chip(kv[-1]))
+    other, kv[-1] = after(other, kv[-1])
     fresh = call(renorm_body, shape((far, 3, part, width), BF16), (half, other, start), 16)
     fresh = lax.all_to_all(fresh, FAR, 0, 0, tiled=True)
     kv.append(next_chip(kv[-1]))

time: 139 us -> 126 us (0.906)
  the two profiles are of different devices: /device:TPU:1 before, /device:TPU:57 now
where the time goes in v3:
time: 126 us
  starting transfers between devices  73.2 us (58%)
  waiting for transfers between devices  34 us (27%)
  Pallas kernels  15 us (12%)
  local copies, waits for them, and re-layouts  2.35 us (2%)
    ppermute x3, starting transfers between devices, next_chip(): return lax.ppermute(value, axes, [(i, i + 2) for i in range(devices - 2)])  18.3 us
    all_to_all x1, starting transfers between devices, on_device(): fw_fine = lax.all_to_all(fw_out, HEAD, 0, 0, tiled=True)  15.3 us
    ppermute x2, starting transfers between devices, swapped(): return lax.ppermute(value, axis, [(0, 1), (1, 0)])  12.1 us
    all_to_all x1, waiting for transfers between devices, on_device(): pieces = lax.all_to_all(pieces, NEAR, 0, 0, tiled=True)  11.8 us
    all_to_all x1, starting transfers between devices, on_device(): pieces = lax.all_to_all(pieces, FAR, 0, 0, tiled=True)  9.12 us
    all_to_all x1, starting transfers between devices, on_device(): fresh = lax.all_to_all(fresh, NEAR, 0, 0, tiled=True)  6.89 us
    all_to_all x1, waiting for transfers between devices, on_device(): fresh = lax.all_to_all(fresh, NEAR, 0, 0, tiled=True)  6.69 us
    pallas_call x1, Pallas kernels, on_device(): pl.pallas_call(grads_body, out_shape=shape((close, far, 3, part, width),...  6.08 us
  transfers between devices with their start and end apart: 10, of which 7 were waited for; matrix products, arithmetic and copies ran while one was open for 2% of the time, Pallas kernels for 4%

profile of v3, /device:TPU:57, one launch (start us, length us, event | category | flops | bytes accessed | tf_op | source)
XLA Modules:
  0.0 125.7 jit_solution(16734616904664501816)
XLA Ops:
  0.0 6.1 %shard_map.82 = bf16[8,4,3,16,512]{4,3,2,1,0:T(8,128)(2,1)} custom-call(bf16[384,512]{1,0:T(8,128)(2,1)} %k_hbm.1, bf16[384,512]{1,0:T(8,128)(2,1)} %v_hbm.1, f32[1,384]{1,0:T(1,128)} %bitcast.9, bf16[3,512,512]{2,1,0:T(8,128)(2,1)} %bitcast.8), custom_call_target="tpu_custom_call" | custom-call | flops 1207959552 | bytes 4194304 | tf_op jit(solution)/shard_map/pallas_call | solution.py:189
  6.1 0.0 copy-start.2
  6.1 0.0 copy-start.3
  6.1 6.0 %all-to-all-start = ((bf16[8,4,3,16,512]{4,3,2,1,0:T(8,128)(2,1)}), bf16[8,4,3,16,512]{4,3,2,1,0:T(8,128)(2,1)S(1)}, u32[]{:S(2)}, u32[]{:S(2)}) async-start(bf16[8,4,3,16,512]{4,3,2,1,0:T(8,128)(2,1)} %shard_map.82), calls=%async_computation | async-start | bytes 3145728 | tf_op jit(solution)/shard_map/all_to_all | solution.py:202
  12.1 0.0 copy-done.2
  12.1 0.0 copy-done.3
  12.1 5.7 %collective-permute-start = (bf16[48,2048]{1,0:T(8,128)(2,1)S(1)}, bf16[48,2048]{1,0:T(8,128)(2,1)S(1)}, u32[]{:S(2)}, u32[]{:S(2)}) collective-permute-start(bf16[48,2048]{1,0:T(8,128)(2,1)S(1)} %constant_dynamic-update-slice_fusion.refs_0_), channel_id=1, source_target_pairs={{0,2},{1,3},{2,4},{3,5},{4,6},{5,7},{6,8},{7,9},{8,10},{9,11},{10,... | collective-permute-start | bytes 589832 | tf_op jit(solution)/shard_map/ppermute | solution.py:32
  17.9 2.9 %collective-permute-done.refs_1_ = bf16[48,2048]{1,0:T(8,128)(2,1)S(1)} collective-permute-done((bf16[48,2048]{1,0:T(8,128)(2,1)S(1)}, bf16[48,2048]{1,0:T(8,128)(2,1)S(1)}, u32[]{:S(2)}, u32[]{:S(2)}) %collective-permute-start) | collective-permute-done | bytes 196640 | tf_op jit(solution)/shard_map/ppermute | solution.py:32
  20.8 11.8 %all-to-all-done.in_ref = bf16[8,4,3,16,512]{4,3,2,1,0:T(8,128)(2,1)S(1)} async-done(((bf16[8,4,3,16,512]{4,3,2,1,0:T(8,128)(2,1)}), bf16[8,4,3,16,512]{4,3,2,1,0:T(8,128)(2,1)S(1)}, u32[]{:S(2)}, u32[]{:S(2)}) %all-to-all-start) | async-done | bytes 1572896 | tf_op jit(solution)/shard_map/all_to_all | solution.py:202
  32.6 0.9 shard_map.83
  33.5 9.1 %all-to-all-start.1 = ((bf16[4,3,16,512]{3,2,1,0:T(8,128)(2,1)}), bf16[4,3,16,512]{3,2,1,0:T(8,128)(2,1)S(1)}, u32[]{:S(2)}, u32[]{:S(2)}) async-start(bf16[4,3,16,512]{3,2,1,0:T(8,128)(2,1)} %shard_map.83), calls=%async_computation.1 | async-start | bytes 393216 | tf_op jit(solution)/shard_map/all_to_all | solution.py:206
  42.6 6.7 %collective-permute-start.2 = (bf16[48,2048]{1,0:T(8,128)(2,1)S(1)}, bf16[48,2048]{1,0:T(8,128)(2,1)S(1)}, u32[]{:S(2)}, u32[]{:S(2)}) collective-permute-start(bf16[48,2048]{1,0:T(8,128)(2,1)S(1)} %collective-permute-done.refs_1_), channel_id=1, source_target_pairs={{0,2},{1,3},{2,4},{3,5},{4,6},{5,7},{6,8},{7,9},{8,10},{9,11},{10,... | collective-permute-start | bytes 589832 | tf_op jit(solution)/shard_map/ppermute | solution.py:32
  49.3 1.1 all-to-all-done.1.in_ref
  50.4 4.4 %collective-permute-start.1 = (f32[3,16,512]{2,1,0:T(8,128)S(1)}, f32[3,16,512]{2,1,0:T(8,128)S(1)}, u32[]{:S(2)}, u32[]{:S(2)}) collective-permute-start(f32[3,16,512]{2,1,0:T(8,128)S(1)} %shard_map.84.half_ref), channel_id=1, source_target_pairs={{0,256},{256,0},{1,257},{257,1},{2,258},{258,2},{3,259},{259,3},{4... | collective-permute-start | bytes 294920 | tf_op jit(solution)/shard_map/ppermute | solution.py:36
  54.9 1.2 constant_dynamic-slice_fusion
  56.1 0.1 copy.9
  56.2 0.0 collective-permute-done.2.refs_2_
  56.2 3.6 %collective-permute-done.1.other_ref = f32[3,16,512]{2,1,0:T(8,128)S(1)} collective-permute-done((f32[3,16,512]{2,1,0:T(8,128)S(1)}, f32[3,16,512]{2,1,0:T(8,128)S(1)}, u32[]{:S(2)}, u32[]{:S(2)}) %collective-permute-start.1) | collective-permute-done | bytes 98336 | tf_op jit(solution)/shard_map/ppermute | solution.py:36
  59.8 0.8 shard_map.85
  60.6 5.6 %all-to-all-start.2 = ((bf16[4,3,16,512]{3,2,1,0:T(8,128)(2,1)}), bf16[4,3,16,512]{3,2,1,0:T(8,128)(2,1)S(1)}, u32[]{:S(2)}, u32[]{:S(2)}) async-start(bf16[4,3,16,512]{3,2,1,0:T(8,128)(2,1)} %shard_map.85), calls=%async_computation.2 | async-start | bytes 393216 | tf_op jit(solution)/shard_map/all_to_all | solution.py:215
  66.2 5.8 %collective-permute-start.3 = (bf16[48,2048]{1,0:T(8,128)(2,1)S(1)}, bf16[48,2048]{1,0:T(8,128)(2,1)S(1)}, u32[]{:S(2)}, u32[]{:S(2)}) collective-permute-start(bf16[48,2048]{1,0:T(8,128)(2,1)S(1)} %collective-permute-done.2.refs_2_), channel_id=1, source_target_pairs={{0,2},{1,3},{2,4},{3,5},{4,6},{5,7},{6,8},{7,9},{8,10},{9,11},{10,... | collective-permute-start | bytes 589832 | tf_op jit(solution)/shard_map/ppermute | solution.py:32
  72.0 2.6 %collective-permute-done.3.refs_3_ = bf16[48,2048]{1,0:T(8,128)(2,1)S(1)} collective-permute-done((bf16[48,2048]{1,0:T(8,128)(2,1)S(1)}, bf16[48,2048]{1,0:T(8,128)(2,1)S(1)}, u32[]{:S(2)}, u32[]{:S(2)}) %collective-permute-start.3) | collective-permute-done | bytes 196640 | tf_op jit(solution)/shard_map/ppermute | solution.py:32
  74.6 0.0 all-to-all-done.2.in_ref
  74.6 1.3 %shard_map.87 = bf16[8,4,3,16,512]{4,3,2,1,0:T(8,128)(2,1)} custom-call(bf16[4,3,16,512]{3,2,1,0:T(8,128)(2,1)S(1)} %all-to-all-done.2.in_ref), custom_call_target="tpu_custom_call" | custom-call | bytes 1769472 | tf_op jit(solution)/shard_map/pallas_call | solution.py:45
  75.9 6.9 %all-to-all-start.3 = ((bf16[8,4,3,16,512]{4,3,2,1,0:T(8,128)(2,1)}), bf16[8,4,3,16,512]{4,3,2,1,0:T(8,128)(2,1)S(1)}, u32[]{:S(2)}, u32[]{:S(2)}) async-start(bf16[8,4,3,16,512]{4,3,2,1,0:T(8,128)(2,1)} %shard_map.87), calls=%async_computation.3 | async-start | bytes 3145728 | tf_op jit(solution)/shard_map/all_to_all | solution.py:219
  82.8 0.0 copy-start
  82.8 1.0 pad_maximum_fusion
  83.7 7.6 %collective-permute-start.4 = (bf16[192,2048]{1,0:T(8,128)(2,1)}, bf16[192,2048]{1,0:T(8,128)(2,1)S(1)}, u32[]{:S(2)}, u32[]{:S(2)}) collective-permute-start(bf16[192,2048]{1,0:T(8,128)(2,1)} %pad_maximum_fusion), channel_id=1, source_target_pairs={{0,1},{1,0},{2,3},{3,2},{4,5},{5,4},{6,7},{7,6},{8,9},{9,8},{10,11... | collective-permute-start | bytes 2359304 | tf_op jit(solution)/shard_map/ppermute | solution.py:36
  91.4 6.7 %all-to-all-done.3.w_ref = bf16[8,4,3,16,512]{4,3,2,1,0:T(8,128)(2,1)S(1)} async-done(((bf16[8,4,3,16,512]{4,3,2,1,0:T(8,128)(2,1)}), bf16[8,4,3,16,512]{4,3,2,1,0:T(8,128)(2,1)S(1)}, u32[]{:S(2)}, u32[]{:S(2)}) %all-to-all-start.3) | async-done | bytes 1572896 | tf_op jit(solution)/shard_map/all_to_all | solution.py:219
  98.1 0.0 copy-done
  98.1 1.6 %shard_map.88 = bf16[8,48,512]{2,1,0:T(8,128)(2,1)} custom-call(bf16[384,512]{1,0:T(8,128)(2,1)S(1)} %copy-done, bf16[8,4,3,16,512]{4,3,2,1,0:T(8,128)(2,1)S(1)} %all-to-all-done.3.w_ref), custom_call_target="tpu_custom_call" | custom-call | flops 603979776 | bytes 2359296 | tf_op jit(solution)/shard_map/pallas_call | solution.py:45
  99.7 15.3 %all-to-all-start.4 = ((bf16[8,48,512]{2,1,0:T(8,128)(2,1)}), bf16[8,48,512]{2,1,0:T(8,128)(2,1)S(1)}, u32[]{:S(2)}, u32[]{:S(2)}) async-start(bf16[8,48,512]{2,1,0:T(8,128)(2,1)} %shard_map.88), calls=%async_computation.4 | async-start | bytes 786432 | tf_op jit(solution)/shard_map/all_to_all | solution.py:229
  115.0 0.1 pad_add_fusion.place_ref
  115.1 0.0 collective-permute-done.4.refs_4_
  115.1 0.0 copy-start.1
  115.1 1.0 copy-done.1
  116.1 3.6 %shard_map.86.attn_ref = f32[48,4096]{1,0:T(8,128)S(1)} custom-call(s32[2]{0:T(128)S(1)} %pad_add_fusion.place_ref, bf16[48,4096]{1,0:T(8,128)(2,1)S(1)} %copy-done.1, bf16[48,2048]{1,0:T(8,128)(2,1)S(1)} %constant_dynamic-update-slice_fusion.refs_0_, bf16[48,2048]{1,0:T(8,128)(2,1)S(1)} %collective-permute-done.refs_1_, ...), custom_call_target="tpu_custom_call" | custom-call | flops 1000000000 | bytes 3145728 | tf_op jit(solution)/shard_map/pallas_call | solution.py:232
  119.7 5.2 %all-to-all-done.4.fw_ref = bf16[8,48,512]{2,1,0:T(8,128)(2,1)S(1)} async-done(((bf16[8,48,512]{2,1,0:T(8,128)(2,1)}), bf16[8,48,512]{2,1,0:T(8,128)(2,1)S(1)}, u32[]{:S(2)}, u32[]{:S(2)}) %all-to-all-start.4) | async-done | bytes 393248 | tf_op jit(solution)/shard_map/all_to_all | solution.py:229
  124.9 0.8 shard_map.89
  (3 shorter events, 0.0 us)
Async XLA Ops:
  6.1 6.0 %copy-start.2 = (bf16[48,1024]{1,0:T(8,128)(2,1)S(1)}, bf16[48,1024]{1,0:T(8,128)(2,1)}, u32[]{:S(2)}) copy-start(bf16[48,1024]{1,0:T(8,128)(2,1)} %param.14) | copy-start | bytes 294916
  6.1 6.0 %copy-start.3 = (bf16[48,1024]{1,0:T(8,128)(2,1)S(1)}, bf16[48,1024]{1,0:T(8,128)(2,1)}, u32[]{:S(2)}) copy-start(bf16[48,1024]{1,0:T(8,128)(2,1)} %param.15) | copy-start | bytes 294916
  6.1 26.5 %all-to-all-start = ((bf16[8,4,3,16,512]{4,3,2,1,0:T(8,128)(2,1)}), bf16[8,4,3,16,512]{4,3,2,1,0:T(8,128)(2,1)S(1)}, u32[]{:S(2)}, u32[]{:S(2)}) async-start(bf16[8,4,3,16,512]{4,3,2,1,0:T(8,128)(2,1)} %shard_map.82), calls=%async_computation | async-start | bytes 3145728 | tf_op jit(solution)/shard_map/all_to_all | solution.py:202
  12.1 8.7 %collective-permute-start = (bf16[48,2048]{1,0:T(8,128)(2,1)S(1)}, bf16[48,2048]{1,0:T(8,128)(2,1)S(1)}, u32[]{:S(2)}, u32[]{:S(2)}) collective-permute-start(bf16[48,2048]{1,0:T(8,128)(2,1)S(1)} %constant_dynamic-update-slice_fusion.refs_0_), channel_id=1, source_target_pairs={{0,2},{1,3},{2,4},{3,5},{4,6},{5,7},{6,8},{7,9},{8,10},{9,11},{10,... | collective-permute-start | bytes 589832 | tf_op jit(solution)/shard_map/ppermute | solution.py:32
  33.5 16.9 %all-to-all-start.1 = ((bf16[4,3,16,512]{3,2,1,0:T(8,128)(2,1)}), bf16[4,3,16,512]{3,2,1,0:T(8,128)(2,1)S(1)}, u32[]{:S(2)}, u32[]{:S(2)}) async-start(bf16[4,3,16,512]{3,2,1,0:T(8,128)(2,1)} %shard_map.83), calls=%async_computation.1 | async-start | bytes 393216 | tf_op jit(solution)/shard_map/all_to_all | solution.py:206
  42.6 13.6 %collective-permute-start.2 = (bf16[48,2048]{1,0:T(8,128)(2,1)S(1)}, bf16[48,2048]{1,0:T(8,128)(2,1)S(1)}, u32[]{:S(2)}, u32[]{:S(2)}) collective-permute-start(bf16[48,2048]{1,0:T(8,128)(2,1)S(1)} %collective-permute-done.refs_1_), channel_id=1, source_target_pairs={{0,2},{1,3},{2,4},{3,5},{4,6},{5,7},{6,8},{7,9},{8,10},{9,11},{10,... | collective-permute-start | bytes 589832 | tf_op jit(solution)/shard_map/ppermute | solution.py:32
  50.4 9.4 %collective-permute-start.1 = (f32[3,16,512]{2,1,0:T(8,128)S(1)}, f32[3,16,512]{2,1,0:T(8,128)S(1)}, u32[]{:S(2)}, u32[]{:S(2)}) collective-permute-start(f32[3,16,512]{2,1,0:T(8,128)S(1)} %shard_map.84.half_ref), channel_id=1, source_target_pairs={{0,256},{256,0},{1,257},{257,1},{2,258},{258,2},{3,259},{259,3},{4... | collective-permute-start | bytes 294920 | tf_op jit(solution)/shard_map/ppermute | solution.py:36
  60.6 14.0 %all-to-all-start.2 = ((bf16[4,3,16,512]{3,2,1,0:T(8,128)(2,1)}), bf16[4,3,16,512]{3,2,1,0:T(8,128)(2,1)S(1)}, u32[]{:S(2)}, u32[]{:S(2)}) async-start(bf16[4,3,16,512]{3,2,1,0:T(8,128)(2,1)} %shard_map.85), calls=%async_computation.2 | async-start | bytes 393216 | tf_op jit(solution)/shard_map/all_to_all | solution.py:215
  66.2 8.4 %collective-permute-start.3 = (bf16[48,2048]{1,0:T(8,128)(2,1)S(1)}, bf16[48,2048]{1,0:T(8,128)(2,1)S(1)}, u32[]{:S(2)}, u32[]{:S(2)}) collective-permute-start(bf16[48,2048]{1,0:T(8,128)(2,1)S(1)} %collective-permute-done.2.refs_2_), channel_id=1, source_target_pairs={{0,2},{1,3},{2,4},{3,5},{4,6},{5,7},{6,8},{7,9},{8,10},{9,11},{10,... | collective-permute-start | bytes 589832 | tf_op jit(solution)/shard_map/ppermute | solution.py:32
  75.9 22.2 %all-to-all-start.3 = ((bf16[8,4,3,16,512]{4,3,2,1,0:T(8,128)(2,1)}), bf16[8,4,3,16,512]{4,3,2,1,0:T(8,128)(2,1)S(1)}, u32[]{:S(2)}, u32[]{:S(2)}) async-start(bf16[8,4,3,16,512]{4,3,2,1,0:T(8,128)(2,1)} %shard_map.87), calls=%async_computation.3 | async-start | bytes 3145728 | tf_op jit(solution)/shard_map/all_to_all | solution.py:219
  82.8 15.3 %copy-start = (bf16[384,512]{1,0:T(8,128)(2,1)S(1)}, bf16[384,512]{1,0:T(8,128)(2,1)}, u32[]{:S(2)}) copy-start(bf16[384,512]{1,0:T(8,128)(2,1)} %q_ref.3) | copy-start | bytes 1179652
  83.7 31.3 %collective-permute-start.4 = (bf16[192,2048]{1,0:T(8,128)(2,1)}, bf16[192,2048]{1,0:T(8,128)(2,1)S(1)}, u32[]{:S(2)}, u32[]{:S(2)}) collective-permute-start(bf16[192,2048]{1,0:T(8,128)(2,1)} %pad_maximum_fusion), channel_id=1, source_target_pairs={{0,1},{1,0},{2,3},{3,2},{4,5},{5,4},{6,7},{7,6},{8,9},{9,8},{10,11... | collective-permute-start | bytes 2359304 | tf_op jit(solution)/shard_map/ppermute | solution.py:36
  99.7 25.2 %all-to-all-start.4 = ((bf16[8,48,512]{2,1,0:T(8,128)(2,1)}), bf16[8,48,512]{2,1,0:T(8,128)(2,1)S(1)}, u32[]{:S(2)}, u32[]{:S(2)}) async-start(bf16[8,48,512]{2,1,0:T(8,128)(2,1)} %shard_map.88), calls=%async_computation.4 | async-start | bytes 786432 | tf_op jit(solution)/shard_map/all_to_all | solution.py:229
  115.1 1.0 copy-start.1

commit v4 on v3

--- a/solution.py
+++ b/solution.py
@@ -54,49 +54,45 @@
     return lax.dot_general(left, right, dims, preferred_element_type=F32)
 
 
-def grads_body(k_hbm, v_hbm, rate_ref, w_hbm, out_ref, k_ref, v_ref, w_ref, sems):
-    close, far, _, part, width = out_ref.shape
-    block = width // 2
+def grads_body(
+    k_hbm, v_hbm, rate_ref, w_hbm, out_hbm, k_ref, v_ref, w_ref, out_ref, in_sems, out_sems
+):
+    close, far, _, part, width = out_hbm.shape
+    sources = (k_hbm, w_hbm.at[0], w_hbm.at[1], v_hbm, w_hbm.at[2])
+    targets = (k_ref, w_ref.at[0], w_ref.at[1], v_ref, w_ref.at[2])
     copies = [
-        pltpu.make_async_copy(source, target, sems.at[i])
-        for i, (source, target) in enumerate(
-            (
-                (k_hbm, k_ref),
-                (w_hbm.at[0], w_ref.at[0]),
-                (w_hbm.at[1], w_ref.at[1]),
-                (v_hbm, v_ref),
-                (w_hbm.at[2], w_ref.at[2]),
-            )
-        )
+        pltpu.make_async_copy(source, target, in_sems.at[i])
+        for i, (source, target) in enumerate(zip(sources, targets))
     ]
     for copy in copies:
         copy.start()
+
+    def send(m, left, right):
+        grad = dot(left, right, ROWS_ROWS).astype(BF16)
+        out_ref[m] = grad.reshape(close, far, part, width)
+        copy = pltpu.make_async_copy(out_ref.at[m], out_hbm.at[:, :, m], out_sems.at[m])
+        copy.start()
+        return copy
+
     copies[0].wait()
     copies[1].wait()
     keys = k_ref[...]
-    for start in range(0, width, block):
-        cols = slice(start, start + block)
-        gate = dot(keys, w_ref[0, :, cols])
-        if start == 0:
-            copies[2].wait()
-        up = dot(keys, w_ref[1, :, cols])
-        if start == 0:
-            copies[3].wait()
-            rates = rate_ref[...].reshape(keys.shape[0], 1)
-            scaled = (rates * v_ref[...].astype(F32)).astype(BF16)
-            copies[4].wait()
-        back = dot(scaled, w_ref[2, cols, :], COLS_COLS)
-        sigm = jax.nn.sigmoid(gate)
-        act = gate * sigm
-        hidden = (act * up).astype(BF16)
-        d_gate = (back * up * sigm * (1.0 + gate * (1.0 - sigm))).astype(BF16)
-        d_up = (back * act).astype(BF16)
-        half = slice(start * close // width, (start + block) * close // width)
-        shape = (close * block // width, far, part, width)
-        out_ref[half, :, 0] = dot(d_gate, keys, ROWS_ROWS).astype(BF16).reshape(shape)
-        out_ref[half, :, 1] = dot(d_up, keys, ROWS_ROWS).astype(BF16).reshape(shape)
-        down = dot(scaled, hidden, ROWS_ROWS).astype(BF16)
-        out_ref[:, :, 2, :, cols] = down.reshape(close, far, part, block)
+    gate = dot(keys, w_ref[0])
+    copies[2].wait()
+    up = dot(keys, w_ref[1])
+    copies[3].wait()
+    rates = rate_ref[...].reshape(keys.shape[0], 1)
+    scaled = (rates * v_ref[...].astype(F32)).astype(BF16)
+    sigm = jax.nn.sigmoid(gate)
+    act = gate * sigm
+    sent = [send(2, scaled, (act * up).astype(BF16))]
+    copies[4].wait()
+    back = dot(scaled, w_ref[2], COLS_COLS)
+    sent.append(send(1, (back * act).astype(BF16), keys))
+    d_gate = (back * up * sigm * (1.0 + gate * (1.0 - sigm))).astype(BF16)
+    sent.append(send(0, d_gate, keys))
+    for copy in sent:
+        copy.wait()
 
 
 def sum_body(in_ref, out_ref):
@@ -190,11 +186,14 @@
         grads_body,
         out_shape=shape((close, far, 3, part, width), BF16),
         in_specs=[hbm, hbm, vmem, hbm],
+        out_specs=hbm,
         scratch_shapes=[
             pltpu.VMEM((tok_rows, width), BF16),
             pltpu.VMEM((tok_rows, width), BF16),
             pltpu.VMEM((3, width, width), BF16),
+            pltpu.VMEM((3, close, far, part, width), BF16),
             pltpu.SemaphoreType.DMA((5,)),
+            pltpu.SemaphoreType.DMA((3,)),
         ],
         compiler_params=pltpu.CompilerParams(vmem_limit_bytes=60 * MIB),
         cost_estimate=pl.CostEstimate(flops=6 * product, bytes_accessed=4 * MIB, transcendentals=0),

time: 126 us -> 126 us (level)
  no operation moved by 1% of the time
where the time goes in v4:
time: 126 us; the launch traced here: 125 us
  starting transfers between devices  73.2 us (58%)
  waiting for transfers between devices  33.9 us (27%)
  Pallas kernels  14.2 us (11%)
  local copies, waits for them, and re-layouts  2.35 us (2%)
    ppermute x3, starting transfers between devices, next_chip(): return lax.ppermute(value, axes, [(i, i + 2) for i in range(devices - 2)])  18.3 us
    all_to_all x1, starting transfers between devices, on_device(): fw_fine = lax.all_to_all(fw_out, HEAD, 0, 0, tiled=True)  15.3 us
    ppermute x2, starting transfers between devices, swapped(): return lax.ppermute(value, axis, [(0, 1), (1, 0)])  12.1 us
    all_to_all x1, waiting for transfers between devices, on_device(): pieces = lax.all_to_all(pieces, NEAR, 0, 0, tiled=True)  11.8 us
    all_to_all x1, starting transfers between devices, on_device(): pieces = lax.all_to_all(pieces, FAR, 0, 0, tiled=True)  9.12 us
    all_to_all x1, starting transfers between devices, on_device(): fresh = lax.all_to_all(fresh, NEAR, 0, 0, tiled=True)  6.89 us
    all_to_all x1, waiting for transfers between devices, on_device(): fresh = lax.all_to_all(fresh, NEAR, 0, 0, tiled=True)  6.69 us
    all_to_all x1, starting transfers between devices, on_device(): pieces = lax.all_to_all(pieces, NEAR, 0, 0, tiled=True)  5.98 us
  transfers between devices with their start and end apart: 10, of which 7 were waited for; matrix products, arithmetic and copies ran while one was open for 2% of the time, Pallas kernels for 4%

profile of v4, /device:TPU:57, one launch (start us, length us, event | category | flops | bytes accessed | tf_op | source)
XLA Modules:
  0.0 124.8 jit_solution(5242360173075075165)
XLA Ops:
  0.0 5.2 %shard_map.82 = bf16[8,4,3,16,512]{4,3,2,1,0:T(8,128)(2,1)} custom-call(bf16[384,512]{1,0:T(8,128)(2,1)} %k_hbm.1, bf16[384,512]{1,0:T(8,128)(2,1)} %v_hbm.1, f32[1,384]{1,0:T(1,128)} %bitcast.9, bf16[3,512,512]{2,1,0:T(8,128)(2,1)} %bitcast.8), custom_call_target="tpu_custom_call" | custom-call | flops 1207959552 | bytes 4194304 | tf_op jit(solution)/shard_map/pallas_call | solution.py:185
  5.3 0.0 copy-start.2
  5.3 0.0 copy-start.3
  5.3 6.0 %all-to-all-start = ((bf16[8,4,3,16,512]{4,3,2,1,0:T(8,128)(2,1)}), bf16[8,4,3,16,512]{4,3,2,1,0:T(8,128)(2,1)S(1)}, u32[]{:S(2)}, u32[]{:S(2)}) async-start(bf16[8,4,3,16,512]{4,3,2,1,0:T(8,128)(2,1)} %shard_map.82), calls=%async_computation | async-start | bytes 3145728 | tf_op jit(solution)/shard_map/all_to_all | solution.py:201
  11.3 0.0 copy-done.2
  11.3 0.0 copy-done.3
  11.3 5.7 %collective-permute-start = (bf16[48,2048]{1,0:T(8,128)(2,1)S(1)}, bf16[48,2048]{1,0:T(8,128)(2,1)S(1)}, u32[]{:S(2)}, u32[]{:S(2)}) collective-permute-start(bf16[48,2048]{1,0:T(8,128)(2,1)S(1)} %constant_dynamic-update-slice_fusion.refs_0_), channel_id=1, source_target_pairs={{0,2},{1,3},{2,4},{3,5},{4,6},{5,7},{6,8},{7,9},{8,10},{9,11},{10,... | collective-permute-start | bytes 589832 | tf_op jit(solution)/shard_map/ppermute | solution.py:32
  17.0 2.9 %collective-permute-done.refs_1_ = bf16[48,2048]{1,0:T(8,128)(2,1)S(1)} collective-permute-done((bf16[48,2048]{1,0:T(8,128)(2,1)S(1)}, bf16[48,2048]{1,0:T(8,128)(2,1)S(1)}, u32[]{:S(2)}, u32[]{:S(2)}) %collective-permute-start) | collective-permute-done | bytes 196640 | tf_op jit(solution)/shard_map/ppermute | solution.py:32
  20.0 11.8 %all-to-all-done.in_ref = bf16[8,4,3,16,512]{4,3,2,1,0:T(8,128)(2,1)S(1)} async-done(((bf16[8,4,3,16,512]{4,3,2,1,0:T(8,128)(2,1)}), bf16[8,4,3,16,512]{4,3,2,1,0:T(8,128)(2,1)S(1)}, u32[]{:S(2)}, u32[]{:S(2)}) %all-to-all-start) | async-done | bytes 1572896 | tf_op jit(solution)/shard_map/all_to_all | solution.py:201
  31.8 0.9 shard_map.83
  32.7 9.1 %all-to-all-start.1 = ((bf16[4,3,16,512]{3,2,1,0:T(8,128)(2,1)}), bf16[4,3,16,512]{3,2,1,0:T(8,128)(2,1)S(1)}, u32[]{:S(2)}, u32[]{:S(2)}) async-start(bf16[4,3,16,512]{3,2,1,0:T(8,128)(2,1)} %shard_map.83), calls=%async_computation.1 | async-start | bytes 393216 | tf_op jit(solution)/shard_map/all_to_all | solution.py:205
  41.8 6.7 %collective-permute-start.2 = (bf16[48,2048]{1,0:T(8,128)(2,1)S(1)}, bf16[48,2048]{1,0:T(8,128)(2,1)S(1)}, u32[]{:S(2)}, u32[]{:S(2)}) collective-permute-start(bf16[48,2048]{1,0:T(8,128)(2,1)S(1)} %collective-permute-done.refs_1_), channel_id=1, source_target_pairs={{0,2},{1,3},{2,4},{3,5},{4,6},{5,7},{6,8},{7,9},{8,10},{9,11},{10,... | collective-permute-start | bytes 589832 | tf_op jit(solution)/shard_map/ppermute | solution.py:32
  48.5 1.1 all-to-all-done.1.in_ref
  49.6 4.4 %collective-permute-start.1 = (f32[3,16,512]{2,1,0:T(8,128)S(1)}, f32[3,16,512]{2,1,0:T(8,128)S(1)}, u32[]{:S(2)}, u32[]{:S(2)}) collective-permute-start(f32[3,16,512]{2,1,0:T(8,128)S(1)} %shard_map.84.half_ref), channel_id=1, source_target_pairs={{0,256},{256,0},{1,257},{257,1},{2,258},{258,2},{3,259},{259,3},{4... | collective-permute-start | bytes 294920 | tf_op jit(solution)/shard_map/ppermute | solution.py:36
  54.1 1.2 constant_dynamic-slice_fusion
  55.2 0.1 copy.9
  55.4 0.0 collective-permute-done.2.refs_2_
  55.4 3.6 %collective-permute-done.1.other_ref = f32[3,16,512]{2,1,0:T(8,128)S(1)} collective-permute-done((f32[3,16,512]{2,1,0:T(8,128)S(1)}, f32[3,16,512]{2,1,0:T(8,128)S(1)}, u32[]{:S(2)}, u32[]{:S(2)}) %collective-permute-start.1) | collective-permute-done | bytes 98336 | tf_op jit(solution)/shard_map/ppermute | solution.py:36
  59.0 0.8 shard_map.85
  59.8 5.6 %all-to-all-start.2 = ((bf16[4,3,16,512]{3,2,1,0:T(8,128)(2,1)}), bf16[4,3,16,512]{3,2,1,0:T(8,128)(2,1)S(1)}, u32[]{:S(2)}, u32[]{:S(2)}) async-start(bf16[4,3,16,512]{3,2,1,0:T(8,128)(2,1)} %shard_map.85), calls=%async_computation.2 | async-start | bytes 393216 | tf_op jit(solution)/shard_map/all_to_all | solution.py:214
  65.3 5.8 %collective-permute-start.3 = (bf16[48,2048]{1,0:T(8,128)(2,1)S(1)}, bf16[48,2048]{1,0:T(8,128)(2,1)S(1)}, u32[]{:S(2)}, u32[]{:S(2)}) collective-permute-start(bf16[48,2048]{1,0:T(8,128)(2,1)S(1)} %collective-permute-done.2.refs_2_), channel_id=1, source_target_pairs={{0,2},{1,3},{2,4},{3,5},{4,6},{5,7},{6,8},{7,9},{8,10},{9,11},{10,... | collective-permute-start | bytes 589832 | tf_op jit(solution)/shard_map/ppermute | solution.py:32
  71.2 2.6 %collective-permute-done.3.refs_3_ = bf16[48,2048]{1,0:T(8,128)(2,1)S(1)} collective-permute-done((bf16[48,2048]{1,0:T(8,128)(2,1)S(1)}, bf16[48,2048]{1,0:T(8,128)(2,1)S(1)}, u32[]{:S(2)}, u32[]{:S(2)}) %collective-permute-start.3) | collective-permute-done | bytes 196640 | tf_op jit(solution)/shard_map/ppermute | solution.py:32
  73.8 0.0 all-to-all-done.2.in_ref
  73.8 1.3 %shard_map.87 = bf16[8,4,3,16,512]{4,3,2,1,0:T(8,128)(2,1)} custom-call(bf16[4,3,16,512]{3,2,1,0:T(8,128)(2,1)S(1)} %all-to-all-done.2.in_ref), custom_call_target="tpu_custom_call" | custom-call | bytes 1769472 | tf_op jit(solution)/shard_map/pallas_call | solution.py:45
  75.1 6.9 %all-to-all-start.3 = ((bf16[8,4,3,16,512]{4,3,2,1,0:T(8,128)(2,1)}), bf16[8,4,3,16,512]{4,3,2,1,0:T(8,128)(2,1)S(1)}, u32[]{:S(2)}, u32[]{:S(2)}) async-start(bf16[8,4,3,16,512]{4,3,2,1,0:T(8,128)(2,1)} %shard_map.87), calls=%async_computation.3 | async-start | bytes 3145728 | tf_op jit(solution)/shard_map/all_to_all | solution.py:218
  81.9 0.0 copy-start
  82.0 1.0 pad_maximum_fusion
  82.9 7.6 %collective-permute-start.4 = (bf16[192,2048]{1,0:T(8,128)(2,1)}, bf16[192,2048]{1,0:T(8,128)(2,1)S(1)}, u32[]{:S(2)}, u32[]{:S(2)}) collective-permute-start(bf16[192,2048]{1,0:T(8,128)(2,1)} %pad_maximum_fusion), channel_id=1, source_target_pairs={{0,1},{1,0},{2,3},{3,2},{4,5},{5,4},{6,7},{7,6},{8,9},{9,8},{10,11... | collective-permute-start | bytes 2359304 | tf_op jit(solution)/shard_map/ppermute | solution.py:36
  90.6 6.7 %all-to-all-done.3.w_ref = bf16[8,4,3,16,512]{4,3,2,1,0:T(8,128)(2,1)S(1)} async-done(((bf16[8,4,3,16,512]{4,3,2,1,0:T(8,128)(2,1)}), bf16[8,4,3,16,512]{4,3,2,1,0:T(8,128)(2,1)S(1)}, u32[]{:S(2)}, u32[]{:S(2)}) %all-to-all-start.3) | async-done | bytes 1572896 | tf_op jit(solution)/shard_map/all_to_all | solution.py:218
  97.3 0.0 copy-done
  97.3 1.6 %shard_map.88 = bf16[8,48,512]{2,1,0:T(8,128)(2,1)} custom-call(bf16[384,512]{1,0:T(8,128)(2,1)S(1)} %copy-done, bf16[8,4,3,16,512]{4,3,2,1,0:T(8,128)(2,1)S(1)} %all-to-all-done.3.w_ref), custom_call_target="tpu_custom_call" | custom-call | flops 603979776 | bytes 2359296 | tf_op jit(solution)/shard_map/pallas_call | solution.py:45
  98.9 15.3 %all-to-all-start.4 = ((bf16[8,48,512]{2,1,0:T(8,128)(2,1)}), bf16[8,48,512]{2,1,0:T(8,128)(2,1)S(1)}, u32[]{:S(2)}, u32[]{:S(2)}) async-start(bf16[8,48,512]{2,1,0:T(8,128)(2,1)} %shard_map.88), calls=%async_computation.4 | async-start | bytes 786432 | tf_op jit(solution)/shard_map/all_to_all | solution.py:228
  114.2 0.1 pad_add_fusion.place_ref
  114.2 0.0 collective-permute-done.4.refs_4_
  114.2 0.0 copy-start.1
  114.2 1.0 copy-done.1
  115.2 3.6 %shard_map.86.attn_ref = f32[48,4096]{1,0:T(8,128)S(1)} custom-call(s32[2]{0:T(128)S(1)} %pad_add_fusion.place_ref, bf16[48,4096]{1,0:T(8,128)(2,1)S(1)} %copy-done.1, bf16[48,2048]{1,0:T(8,128)(2,1)S(1)} %constant_dynamic-update-slice_fusion.refs_0_, bf16[48,2048]{1,0:T(8,128)(2,1)S(1)} %collective-permute-done.refs_1_, ...), custom_call_target="tpu_custom_call" | custom-call | flops 1000000000 | bytes 3145728 | tf_op jit(solution)/shard_map/pallas_call | solution.py:231
  118.8 5.2 %all-to-all-done.4.fw_ref = bf16[8,48,512]{2,1,0:T(8,128)(2,1)S(1)} async-done(((bf16[8,48,512]{2,1,0:T(8,128)(2,1)}), bf16[8,48,512]{2,1,0:T(8,128)(2,1)S(1)}, u32[]{:S(2)}, u32[]{:S(2)}) %all-to-all-start.4) | async-done | bytes 393248 | tf_op jit(solution)/shard_map/all_to_all | solution.py:228
  124.0 0.8 shard_map.89
  (3 shorter events, 0.0 us)
Async XLA Ops:
  5.3 6.0 %copy-start.2 = (bf16[48,1024]{1,0:T(8,128)(2,1)S(1)}, bf16[48,1024]{1,0:T(8,128)(2,1)}, u32[]{:S(2)}) copy-start(bf16[48,1024]{1,0:T(8,128)(2,1)} %param.14) | copy-start | bytes 294916
  5.3 6.0 %copy-start.3 = (bf16[48,1024]{1,0:T(8,128)(2,1)S(1)}, bf16[48,1024]{1,0:T(8,128)(2,1)}, u32[]{:S(2)}) copy-start(bf16[48,1024]{1,0:T(8,128)(2,1)} %param.15) | copy-start | bytes 294916
  5.3 26.5 %all-to-all-start = ((bf16[8,4,3,16,512]{4,3,2,1,0:T(8,128)(2,1)}), bf16[8,4,3,16,512]{4,3,2,1,0:T(8,128)(2,1)S(1)}, u32[]{:S(2)}, u32[]{:S(2)}) async-start(bf16[8,4,3,16,512]{4,3,2,1,0:T(8,128)(2,1)} %shard_map.82), calls=%async_computation | async-start | bytes 3145728 | tf_op jit(solution)/shard_map/all_to_all | solution.py:201
  11.3 8.7 %collective-permute-start = (bf16[48,2048]{1,0:T(8,128)(2,1)S(1)}, bf16[48,2048]{1,0:T(8,128)(2,1)S(1)}, u32[]{:S(2)}, u32[]{:S(2)}) collective-permute-start(bf16[48,2048]{1,0:T(8,128)(2,1)S(1)} %constant_dynamic-update-slice_fusion.refs_0_), channel_id=1, source_target_pairs={{0,2},{1,3},{2,4},{3,5},{4,6},{5,7},{6,8},{7,9},{8,10},{9,11},{10,... | collective-permute-start | bytes 589832 | tf_op jit(solution)/shard_map/ppermute | solution.py:32
  32.7 16.9 %all-to-all-start.1 = ((bf16[4,3,16,512]{3,2,1,0:T(8,128)(2,1)}), bf16[4,3,16,512]{3,2,1,0:T(8,128)(2,1)S(1)}, u32[]{:S(2)}, u32[]{:S(2)}) async-start(bf16[4,3,16,512]{3,2,1,0:T(8,128)(2,1)} %shard_map.83), calls=%async_computation.1 | async-start | bytes 393216 | tf_op jit(solution)/shard_map/all_to_all | solution.py:205
  41.8 13.6 %collective-permute-start.2 = (bf16[48,2048]{1,0:T(8,128)(2,1)S(1)}, bf16[48,2048]{1,0:T(8,128)(2,1)S(1)}, u32[]{:S(2)}, u32[]{:S(2)}) collective-permute-start(bf16[48,2048]{1,0:T(8,128)(2,1)S(1)} %collective-permute-done.refs_1_), channel_id=1, source_target_pairs={{0,2},{1,3},{2,4},{3,5},{4,6},{5,7},{6,8},{7,9},{8,10},{9,11},{10,... | collective-permute-start | bytes 589832 | tf_op jit(solution)/shard_map/ppermute | solution.py:32
  49.6 9.4 %collective-permute-start.1 = (f32[3,16,512]{2,1,0:T(8,128)S(1)}, f32[3,16,512]{2,1,0:T(8,128)S(1)}, u32[]{:S(2)}, u32[]{:S(2)}) collective-permute-start(f32[3,16,512]{2,1,0:T(8,128)S(1)} %shard_map.84.half_ref), channel_id=1, source_target_pairs={{0,256},{256,0},{1,257},{257,1},{2,258},{258,2},{3,259},{259,3},{4... | collective-permute-start | bytes 294920 | tf_op jit(solution)/shard_map/ppermute | solution.py:36
  59.8 14.0 %all-to-all-start.2 = ((bf16[4,3,16,512]{3,2,1,0:T(8,128)(2,1)}), bf16[4,3,16,512]{3,2,1,0:T(8,128)(2,1)S(1)}, u32[]{:S(2)}, u32[]{:S(2)}) async-start(bf16[4,3,16,512]{3,2,1,0:T(8,128)(2,1)} %shard_map.85), calls=%async_computation.2 | async-start | bytes 393216 | tf_op jit(solution)/shard_map/all_to_all | solution.py:214
  65.3 8.4 %collective-permute-start.3 = (bf16[48,2048]{1,0:T(8,128)(2,1)S(1)}, bf16[48,2048]{1,0:T(8,128)(2,1)S(1)}, u32[]{:S(2)}, u32[]{:S(2)}) collective-permute-start(bf16[48,2048]{1,0:T(8,128)(2,1)S(1)} %collective-permute-done.2.refs_2_), channel_id=1, source_target_pairs={{0,2},{1,3},{2,4},{3,5},{4,6},{5,7},{6,8},{7,9},{8,10},{9,11},{10,... | collective-permute-start | bytes 589832 | tf_op jit(solution)/shard_map/ppermute | solution.py:32
  75.1 22.2 %all-to-all-start.3 = ((bf16[8,4,3,16,512]{4,3,2,1,0:T(8,128)(2,1)}), bf16[8,4,3,16,512]{4,3,2,1,0:T(8,128)(2,1)S(1)}, u32[]{:S(2)}, u32[]{:S(2)}) async-start(bf16[8,4,3,16,512]{4,3,2,1,0:T(8,128)(2,1)} %shard_map.87), calls=%async_computation.3 | async-start | bytes 3145728 | tf_op jit(solution)/shard_map/all_to_all | solution.py:218
  81.9 15.3 %copy-start = (bf16[384,512]{1,0:T(8,128)(2,1)S(1)}, bf16[384,512]{1,0:T(8,128)(2,1)}, u32[]{:S(2)}) copy-start(bf16[384,512]{1,0:T(8,128)(2,1)} %q_ref.3) | copy-start | bytes 1179652
  82.9 31.3 %collective-permute-start.4 = (bf16[192,2048]{1,0:T(8,128)(2,1)}, bf16[192,2048]{1,0:T(8,128)(2,1)S(1)}, u32[]{:S(2)}, u32[]{:S(2)}) collective-permute-start(bf16[192,2048]{1,0:T(8,128)(2,1)} %pad_maximum_fusion), channel_id=1, source_target_pairs={{0,1},{1,0},{2,3},{3,2},{4,5},{5,4},{6,7},{7,6},{8,9},{9,8},{10,11... | collective-permute-start | bytes 2359304 | tf_op jit(solution)/shard_map/ppermute | solution.py:36
  98.9 25.2 %all-to-all-start.4 = ((bf16[8,48,512]{2,1,0:T(8,128)(2,1)}), bf16[8,48,512]{2,1,0:T(8,128)(2,1)S(1)}, u32[]{:S(2)}, u32[]{:S(2)}) async-start(bf16[8,48,512]{2,1,0:T(8,128)(2,1)} %shard_map.88), calls=%async_computation.4 | async-start | bytes 786432 | tf_op jit(solution)/shard_map/all_to_all | solution.py:228
  114.2 1.0 copy-start.1

commit v5 on v4

--- a/solution.py
+++ b/solution.py
@@ -26,10 +26,16 @@
 COLS_COLS = (((1,), (1,)), ((), ()))
 
 
-def next_chip(value):
-    axes = SEQ + HEAD
-    devices = lax.axis_size(axes)
-    return lax.ppermute(value, axes, [(i, i + 2) for i in range(devices - 2)])
+def next_step(value):
+    steps = lax.axis_size(SEQ)
+    return lax.ppermute(value, SEQ, [(i, i + 1) for i in range(steps - 1)])
+
+
+def across(own, before, away):
+    chips = lax.axis_size("yl")
+    place = lax.axis_index("yl")
+    block = jnp.where((place ^ away) > place, own, before)
+    return lax.ppermute(block, "yl", [(i, i ^ away) for i in range(chips)])
 
 
 def swapped(value, axis):
@@ -135,12 +141,11 @@
     span = 2 * links * rows
     group = Q_HEADS // KV_HEADS
     kv_width = KV_HEADS * HEAD_DIM
-    device, other = place_ref[0], place_ref[1]
+    device = place_ref[0]
     key = lax.broadcasted_iota(jnp.int32, (1, span), 1)
-    s_pos = key + device * rows
+    s_pos = key + place_ref[0] * rows
     for i in range(1, 2 * links):
-        origin = device - 2 * i if i < links else other - 2 * (i - links)
-        s_pos = jnp.where(key >= i * rows, key + (origin - i) * rows, s_pos)
+        s_pos = jnp.where(key >= i * rows, key + (place_ref[i] - i) * rows, s_pos)
     t_pos = device * rows + lax.broadcasted_iota(jnp.int32, (rows, 1), 0)
     gap = t_pos - s_pos
     keep = (gap >= 0) & (gap < WINDOW) & (s_pos >= 0)
@@ -199,8 +204,8 @@
         cost_estimate=pl.CostEstimate(flops=6 * product, bytes_accessed=4 * MIB, transcendentals=0),
     )(fw_key, fw_value, learn_rate.reshape(1, tok_rows), weights)
     pieces = lax.all_to_all(pieces, NEAR, 0, 0, tiled=True)
-    kv.append(next_chip(kv[-1]))
-    pieces, kv[-1] = after(pieces, kv[-1])
+    before = next_step(kv[0])
+    pieces, before = after(pieces, before)
     pieces = call(sum_body, shape((far, 3, part, width), BF16), (pieces,), 16)
     pieces = lax.all_to_all(pieces, FAR, 0, 0, tiled=True)
     half = call(sum_body, shape((3, part, width), F32), (pieces,), 16)
@@ -208,14 +213,15 @@
     mine = (lax.axis_index(NEAR) * far + lax.axis_index(FAR)) * part
     start = lax.dynamic_slice_in_dim(weights, mine, part, 2).transpose(0, 2, 1)
     other = swapped(half, "yh")
-    kv.append(next_chip(kv[-1]))
-    other, kv[-1] = after(other, kv[-1])
+    kv += [across(kv[0], before, 1)]
+    other, kv[-1:] = after(other, kv[-1:])
     fresh = call(renorm_body, shape((far, 3, part, width), BF16), (half, other, start), 16)
     fresh = lax.all_to_all(fresh, FAR, 0, 0, tiled=True)
-    kv.append(next_chip(kv[-1]))
-    fresh, kv[-1] = after(fresh, kv[-1])
+    kv += [across(kv[0], before, 2)]
+    fresh, kv[-1:] = after(fresh, kv[-1:])
     fresh = call(copies_body, shape((close, far, 3, part, width), BF16), (fresh,), 16)
     fresh = lax.all_to_all(fresh, NEAR, 0, 0, tiled=True)
+    kv += [across(kv[0], before, 3)]
     swap = swapped(jnp.concatenate(kv), "core")
 
     fw_out = call(
@@ -226,8 +232,17 @@
         3 * product,
     )
     fw_fine = lax.all_to_all(fw_out, HEAD, 0, 0, tiled=True)
-    device = lax.axis_index(SEQ + HEAD)
-    place = jnp.stack([device, device + 1 - 2 * lax.axis_index("core")])
+    chip, core = lax.axis_index("yl"), lax.axis_index("core")
+    heads = lax.axis_size(HEAD)
+    place = jnp.stack(
+        [
+            (lax.axis_index(SEQ) - ((chip ^ away) > chip).astype(jnp.int32)) * heads
+            + 2 * (chip ^ away)
+            + side
+            for side in (core, 1 - core)
+            for away in range(4)
+        ]
+    )
     attn = pl.pallas_call(
         attend_body,
         out_shape=shape(attn_query.shape, F32),

time: 126 us -> 124 us (0.984)
  starting transfers between devices: 73.2 us -> 58.1 us
  waiting for transfers between devices: 33.9 us -> 46.6 us
    ppermute x3 -> x4, waiting for transfers between devices: 5.54 us -> 28 us  [the longest x1 17.2 us: next_step(): return lax.ppermute(value, SEQ, [(i, i + 1) for i in range(steps - 1)])]
    all_to_all x1, waiting for transfers between devices: 11.8 us -> 4.08 us  [on_device(): pieces = lax.all_to_all(pieces, NEAR, 0, 0, tiled=True)]
    all_to_all x1, waiting for transfers between devices: 6.69 us -> 0.01 us  [on_device(): fresh = lax.all_to_all(fresh, NEAR, 0, 0, tiled=True)]
    all_to_all x1, starting transfers between devices: 15.3 us -> 8.88 us  [on_device(): fw_fine = lax.all_to_all(fw_out, HEAD, 0, 0, tiled=True)]
    ppermute x3 -> x4, starting transfers between devices: 18.3 us -> 13.6 us  [the longest x3 10.3 us: across(): return lax.ppermute(block, 'yl', [(i, i ^ away) for i in range(chips)])]
    all_to_all x1, waiting for transfers between devices: 1.1 us -> 4.74 us  [on_device(): pieces = lax.all_to_all(pieces, FAR, 0, 0, tiled=True)]
    all_to_all x1, starting transfers between devices: 6.89 us -> 4.12 us  [on_device(): fresh = lax.all_to_all(fresh, NEAR, 0, 0, tiled=True)]
    all_to_all x1, starting transfers between devices: 5.55 us -> 3.37 us  [on_device(): fresh = lax.all_to_all(fresh, FAR, 0, 0, tiled=True)]
  transfers between devices with their start and end apart: 10 -> 11, of which waited for: 7 -> 7; matrix products, arithmetic and copies ran while one was open for 2% -> 2% of each run, Pallas kernels for 4% -> 4%
where the time goes in v5:
time: 124 us; the launch traced here: 122 us
  starting transfers between devices  58.1 us (47%)
  waiting for transfers between devices  46.6 us (38%)
  Pallas kernels  14.2 us (11%)
  local copies, waits for them, and re-layouts  2.43 us (2%)
    ppermute x1, waiting for transfers between devices, next_step(): return lax.ppermute(value, SEQ, [(i, i + 1) for i in range(steps - 1)])  17.2 us
    ppermute x2, starting transfers between devices, swapped(): return lax.ppermute(value, axis, [(0, 1), (1, 0)])  13.1 us
    ppermute x3, waiting for transfers between devices, across(): return lax.ppermute(block, 'yl', [(i, i ^ away) for i in range(chips)])  10.8 us
    ppermute x3, starting transfers between devices, across(): return lax.ppermute(block, 'yl', [(i, i ^ away) for i in range(chips)])  10.3 us
    all_to_all x1, starting transfers between devices, on_device(): pieces = lax.all_to_all(pieces, FAR, 0, 0, tiled=True)  9.12 us
    all_to_all x1, starting transfers between devices, on_device(): fw_fine = lax.all_to_all(fw_out, HEAD, 0, 0, tiled=True)  8.88 us
    all_to_all x1, starting transfers between devices, on_device(): pieces = lax.all_to_all(pieces, NEAR, 0, 0, tiled=True)  5.98 us
    pallas_call x6, Pallas kernels, call(): pl.pallas_call(body, out_shape=out, compiler_params=pltpu.CompilerParams(...  5.39 us
  transfers between devices with their start and end apart: 11, of which 7 were waited for; matrix products, arithmetic and copies ran while one was open for 2% of the time, Pallas kernels for 4%

profile of v5, /device:TPU:57, one launch (start us, length us, event | category | flops | bytes accessed | tf_op | source)
XLA Modules:
  0.0 122.5 jit_solution(7424365333444947497)
XLA Ops:
  0.0 5.2 %shard_map.82 = bf16[8,4,3,16,512]{4,3,2,1,0:T(8,128)(2,1)} custom-call(bf16[384,512]{1,0:T(8,128)(2,1)} %k_hbm.1, bf16[384,512]{1,0:T(8,128)(2,1)} %v_hbm.1, f32[1,384]{1,0:T(1,128)} %bitcast.15, bf16[3,512,512]{2,1,0:T(8,128)(2,1)} %bitcast.14), custom_call_target="tpu_custom_call" | custom-call | flops 1207959552 | bytes 4194304 | tf_op jit(solution)/shard_map/pallas_call | solution.py:190
  5.2 0.0 copy-start.2
  5.3 0.0 copy-start.3
  5.3 6.0 %all-to-all-start = ((bf16[8,4,3,16,512]{4,3,2,1,0:T(8,128)(2,1)}), bf16[8,4,3,16,512]{4,3,2,1,0:T(8,128)(2,1)S(1)}, u32[]{:S(2)}, u32[]{:S(2)}) async-start(bf16[8,4,3,16,512]{4,3,2,1,0:T(8,128)(2,1)} %shard_map.82), calls=%async_computation | async-start | bytes 3145728 | tf_op jit(solution)/shard_map/all_to_all | solution.py:206
  11.2 0.0 copy-done.2
  11.3 0.0 copy-done.3
  11.3 3.4 %collective-permute-start = (bf16[48,2048]{1,0:T(8,128)(2,1)S(1)}, bf16[48,2048]{1,0:T(8,128)(2,1)S(1)}, u32[]{:S(2)}, u32[]{:S(2)}) collective-permute-start(bf16[48,2048]{1,0:T(8,128)(2,1)S(1)} %constant_dynamic-update-slice_fusion.refs_0_), channel_id=1, source_target_pairs={{0,8},{8,16},{16,24},{24,32},{32,40},{40,48},{48,56},{56,64},{64,7... | collective-permute-start | bytes 589832 | tf_op jit(solution)/shard_map/ppermute | solution.py:31
  14.7 17.2 %collective-permute-done = bf16[48,2048]{1,0:T(8,128)(2,1)S(1)} collective-permute-done((bf16[48,2048]{1,0:T(8,128)(2,1)S(1)}, bf16[48,2048]{1,0:T(8,128)(2,1)S(1)}, u32[]{:S(2)}, u32[]{:S(2)}) %collective-permute-start) | collective-permute-done | bytes 196640 | tf_op jit(solution)/shard_map/ppermute | solution.py:31
  31.9 4.1 %all-to-all-done.in_ref = bf16[8,4,3,16,512]{4,3,2,1,0:T(8,128)(2,1)S(1)} async-done(((bf16[8,4,3,16,512]{4,3,2,1,0:T(8,128)(2,1)}), bf16[8,4,3,16,512]{4,3,2,1,0:T(8,128)(2,1)S(1)}, u32[]{:S(2)}, u32[]{:S(2)}) %all-to-all-start) | async-done | bytes 1572896 | tf_op jit(solution)/shard_map/all_to_all | solution.py:206
  36.0 0.9 shard_map.83
  36.9 9.1 %all-to-all-start.1 = ((bf16[4,3,16,512]{3,2,1,0:T(8,128)(2,1)}), bf16[4,3,16,512]{3,2,1,0:T(8,128)(2,1)S(1)}, u32[]{:S(2)}, u32[]{:S(2)}) async-start(bf16[4,3,16,512]{3,2,1,0:T(8,128)(2,1)} %shard_map.83), calls=%async_computation.1 | async-start | bytes 393216 | tf_op jit(solution)/shard_map/all_to_all | solution.py:210
  46.0 3.0 %collective-permute-start.2 = (bf16[48,2048]{1,0:T(8,128)(2,1)S(1)}, bf16[48,2048]{1,0:T(8,128)(2,1)S(1)}, u32[]{:S(2)}, u32[]{:S(2)}) collective-permute-start(bf16[48,2048]{1,0:T(8,128)(2,1)S(1)} %get-tuple-element.19), channel_id=1, source_target_pairs={{0,2},{2,0},{4,6},{6,4},{1,3},{3,1},{5,7},{7,5},{8,10},{10,8},{12,... | collective-permute-start | bytes 589832 | tf_op jit(solution)/shard_map/ppermute | solution.py:38
  49.0 4.7 %all-to-all-done.1.in_ref = bf16[4,3,16,512]{3,2,1,0:T(8,128)(2,1)S(1)} async-done(((bf16[4,3,16,512]{3,2,1,0:T(8,128)(2,1)}), bf16[4,3,16,512]{3,2,1,0:T(8,128)(2,1)S(1)}, u32[]{:S(2)}, u32[]{:S(2)}) %all-to-all-start.1) | async-done | bytes 196640 | tf_op jit(solution)/shard_map/all_to_all | solution.py:210
  53.8 4.4 %collective-permute-start.1 = (f32[3,16,512]{2,1,0:T(8,128)S(1)}, f32[3,16,512]{2,1,0:T(8,128)S(1)}, u32[]{:S(2)}, u32[]{:S(2)}) collective-permute-start(f32[3,16,512]{2,1,0:T(8,128)S(1)} %shard_map.84.half_ref), channel_id=1, source_target_pairs={{0,256},{256,0},{1,257},{257,1},{2,258},{258,2},{3,259},{259,3},{4... | collective-permute-start | bytes 294920 | tf_op jit(solution)/shard_map/ppermute | solution.py:42
  58.2 1.2 constant_dynamic-slice_fusion
  59.4 0.1 copy.9
  59.6 0.0 collective-permute-done.2.refs_1_
  59.6 4.5 %collective-permute-done.1.other_ref = f32[3,16,512]{2,1,0:T(8,128)S(1)} collective-permute-done((f32[3,16,512]{2,1,0:T(8,128)S(1)}, f32[3,16,512]{2,1,0:T(8,128)S(1)}, u32[]{:S(2)}, u32[]{:S(2)}) %collective-permute-start.1) | collective-permute-done | bytes 98336 | tf_op jit(solution)/shard_map/ppermute | solution.py:42
  64.1 0.8 shard_map.85
  64.9 3.4 %all-to-all-start.2 = ((bf16[4,3,16,512]{3,2,1,0:T(8,128)(2,1)}), bf16[4,3,16,512]{3,2,1,0:T(8,128)(2,1)S(1)}, u32[]{:S(2)}, u32[]{:S(2)}) async-start(bf16[4,3,16,512]{3,2,1,0:T(8,128)(2,1)} %shard_map.85), calls=%async_computation.2 | async-start | bytes 393216 | tf_op jit(solution)/shard_map/all_to_all | solution.py:219
  68.3 3.1 %collective-permute-start.3 = (bf16[48,2048]{1,0:T(8,128)(2,1)S(1)}, bf16[48,2048]{1,0:T(8,128)(2,1)S(1)}, u32[]{:S(2)}, u32[]{:S(2)}) collective-permute-start(bf16[48,2048]{1,0:T(8,128)(2,1)S(1)} %get-tuple-element.18), channel_id=1, source_target_pairs={{0,4},{2,6},{4,0},{6,2},{1,5},{3,7},{5,1},{7,3},{8,12},{10,14},{12... | collective-permute-start | bytes 589832 | tf_op jit(solution)/shard_map/ppermute | solution.py:38
  71.4 6.6 %collective-permute-done.3.refs_2_ = bf16[48,2048]{1,0:T(8,128)(2,1)S(1)} collective-permute-done((bf16[48,2048]{1,0:T(8,128)(2,1)S(1)}, bf16[48,2048]{1,0:T(8,128)(2,1)S(1)}, u32[]{:S(2)}, u32[]{:S(2)}) %collective-permute-start.3) | collective-permute-done | bytes 196640 | tf_op jit(solution)/shard_map/ppermute | solution.py:38
  78.0 0.0 all-to-all-done.2.in_ref
  78.0 1.3 %shard_map.87 = bf16[8,4,3,16,512]{4,3,2,1,0:T(8,128)(2,1)} custom-call(bf16[4,3,16,512]{3,2,1,0:T(8,128)(2,1)S(1)} %all-to-all-done.2.in_ref), custom_call_target="tpu_custom_call" | custom-call | bytes 1769472 | tf_op jit(solution)/shard_map/pallas_call | solution.py:51
  79.3 4.1 %all-to-all-start.3 = ((bf16[8,4,3,16,512]{4,3,2,1,0:T(8,128)(2,1)}), bf16[8,4,3,16,512]{4,3,2,1,0:T(8,128)(2,1)S(1)}, u32[]{:S(2)}, u32[]{:S(2)}) async-start(bf16[8,4,3,16,512]{4,3,2,1,0:T(8,128)(2,1)} %shard_map.87), calls=%async_computation.3 | async-start | bytes 3145728 | tf_op jit(solution)/shard_map/all_to_all | solution.py:223
  83.4 0.0 copy-start
  83.4 4.2 %collective-permute-start.4 = (bf16[48,2048]{1,0:T(8,128)(2,1)S(1)}, bf16[48,2048]{1,0:T(8,128)(2,1)S(1)}, u32[]{:S(2)}, u32[]{:S(2)}) collective-permute-start(bf16[48,2048]{1,0:T(8,128)(2,1)S(1)} %get-tuple-element.17), channel_id=1, source_target_pairs={{0,6},{2,4},{4,2},{6,0},{1,7},{3,5},{5,3},{7,1},{8,14},{10,12},{12... | collective-permute-start | bytes 589832 | tf_op jit(solution)/shard_map/ppermute | solution.py:38
  87.6 4.2 %collective-permute-done.4.refs_3_ = bf16[48,2048]{1,0:T(8,128)(2,1)S(1)} collective-permute-done((bf16[48,2048]{1,0:T(8,128)(2,1)S(1)}, bf16[48,2048]{1,0:T(8,128)(2,1)S(1)}, u32[]{:S(2)}, u32[]{:S(2)}) %collective-permute-start.4) | collective-permute-done | bytes 196640 | tf_op jit(solution)/shard_map/ppermute | solution.py:38
  91.7 0.9 pad_maximum_fusion
  92.7 8.6 %collective-permute-start.5 = (bf16[192,2048]{1,0:T(8,128)(2,1)}, bf16[192,2048]{1,0:T(8,128)(2,1)S(1)}, u32[]{:S(2)}, u32[]{:S(2)}) collective-permute-start(bf16[192,2048]{1,0:T(8,128)(2,1)} %pad_maximum_fusion), channel_id=1, source_target_pairs={{0,1},{1,0},{2,3},{3,2},{4,5},{5,4},{6,7},{7,6},{8,9},{9,8},{10,11... | collective-permute-start | bytes 2359304 | tf_op jit(solution)/shard_map/ppermute | solution.py:42
  101.3 0.0 all-to-all-done.3.w_ref
  101.3 0.0 copy-done
  101.3 1.6 %shard_map.88 = bf16[8,48,512]{2,1,0:T(8,128)(2,1)} custom-call(bf16[384,512]{1,0:T(8,128)(2,1)S(1)} %copy-done, bf16[8,4,3,16,512]{4,3,2,1,0:T(8,128)(2,1)S(1)} %all-to-all-done.3.w_ref), custom_call_target="tpu_custom_call" | custom-call | flops 603979776 | bytes 2359296 | tf_op jit(solution)/shard_map/pallas_call | solution.py:51
  102.9 8.9 %all-to-all-start.4 = ((bf16[8,48,512]{2,1,0:T(8,128)(2,1)}), bf16[8,48,512]{2,1,0:T(8,128)(2,1)S(1)}, u32[]{:S(2)}, u32[]{:S(2)}) async-start(bf16[8,48,512]{2,1,0:T(8,128)(2,1)} %shard_map.88), calls=%async_computation.4 | async-start | bytes 786432 | tf_op jit(solution)/shard_map/all_to_all | solution.py:234
  111.8 0.1 stack.35.place_ref
  111.9 0.0 collective-permute-done.5.refs_4_
  111.9 0.0 copy-start.1
  111.9 1.0 copy-done.1
  112.9 3.6 %shard_map.86.attn_ref = f32[48,4096]{1,0:T(8,128)S(1)} custom-call(s32[8]{0:T(128)S(1)} %stack.35.place_ref, bf16[48,4096]{1,0:T(8,128)(2,1)S(1)} %copy-done.1, bf16[48,2048]{1,0:T(8,128)(2,1)S(1)} %constant_dynamic-update-slice_fusion.refs_0_, bf16[48,2048]{1,0:T(8,128)(2,1)S(1)} %collective-permute-done.2.refs_1_, ...), custom_call_target="tpu_custom_call" | custom-call | flops 1000000000 | bytes 3145728 | tf_op jit(solution)/shard_map/pallas_call | solution.py:246
  116.5 5.2 %all-to-all-done.4.fw_ref = bf16[8,48,512]{2,1,0:T(8,128)(2,1)S(1)} async-done(((bf16[8,48,512]{2,1,0:T(8,128)(2,1)}), bf16[8,48,512]{2,1,0:T(8,128)(2,1)S(1)}, u32[]{:S(2)}, u32[]{:S(2)}) %all-to-all-start.4) | async-done | bytes 393248 | tf_op jit(solution)/shard_map/all_to_all | solution.py:234
  121.7 0.8 shard_map.89
  (4 shorter events, 0.1 us)
Async XLA Ops:
  5.2 6.0 %copy-start.2 = (bf16[48,1024]{1,0:T(8,128)(2,1)S(1)}, bf16[48,1024]{1,0:T(8,128)(2,1)}, u32[]{:S(2)}) copy-start(bf16[48,1024]{1,0:T(8,128)(2,1)} %param.14) | copy-start | bytes 294916
  5.3 6.0 %copy-start.3 = (bf16[48,1024]{1,0:T(8,128)(2,1)S(1)}, bf16[48,1024]{1,0:T(8,128)(2,1)}, u32[]{:S(2)}) copy-start(bf16[48,1024]{1,0:T(8,128)(2,1)} %param.15) | copy-start | bytes 294916
  5.3 30.7 %all-to-all-start = ((bf16[8,4,3,16,512]{4,3,2,1,0:T(8,128)(2,1)}), bf16[8,4,3,16,512]{4,3,2,1,0:T(8,128)(2,1)S(1)}, u32[]{:S(2)}, u32[]{:S(2)}) async-start(bf16[8,4,3,16,512]{4,3,2,1,0:T(8,128)(2,1)} %shard_map.82), calls=%async_computation | async-start | bytes 3145728 | tf_op jit(solution)/shard_map/all_to_all | solution.py:206
  11.3 20.6 %collective-permute-start = (bf16[48,2048]{1,0:T(8,128)(2,1)S(1)}, bf16[48,2048]{1,0:T(8,128)(2,1)S(1)}, u32[]{:S(2)}, u32[]{:S(2)}) collective-permute-start(bf16[48,2048]{1,0:T(8,128)(2,1)S(1)} %constant_dynamic-update-slice_fusion.refs_0_), channel_id=1, source_target_pairs={{0,8},{8,16},{16,24},{24,32},{32,40},{40,48},{48,56},{56,64},{64,7... | collective-permute-start | bytes 589832 | tf_op jit(solution)/shard_map/ppermute | solution.py:31
  36.9 16.9 %all-to-all-start.1 = ((bf16[4,3,16,512]{3,2,1,0:T(8,128)(2,1)}), bf16[4,3,16,512]{3,2,1,0:T(8,128)(2,1)S(1)}, u32[]{:S(2)}, u32[]{:S(2)}) async-start(bf16[4,3,16,512]{3,2,1,0:T(8,128)(2,1)} %shard_map.83), calls=%async_computation.1 | async-start | bytes 393216 | tf_op jit(solution)/shard_map/all_to_all | solution.py:210
  46.0 13.5 %collective-permute-start.2 = (bf16[48,2048]{1,0:T(8,128)(2,1)S(1)}, bf16[48,2048]{1,0:T(8,128)(2,1)S(1)}, u32[]{:S(2)}, u32[]{:S(2)}) collective-permute-start(bf16[48,2048]{1,0:T(8,128)(2,1)S(1)} %get-tuple-element.19), channel_id=1, source_target_pairs={{0,2},{2,0},{4,6},{6,4},{1,3},{3,1},{5,7},{7,5},{8,10},{10,8},{12,... | collective-permute-start | bytes 589832 | tf_op jit(solution)/shard_map/ppermute | solution.py:38
  53.8 10.3 %collective-permute-start.1 = (f32[3,16,512]{2,1,0:T(8,128)S(1)}, f32[3,16,512]{2,1,0:T(8,128)S(1)}, u32[]{:S(2)}, u32[]{:S(2)}) collective-permute-start(f32[3,16,512]{2,1,0:T(8,128)S(1)} %shard_map.84.half_ref), channel_id=1, source_target_pairs={{0,256},{256,0},{1,257},{257,1},{2,258},{258,2},{3,259},{259,3},{4... | collective-permute-start | bytes 294920 | tf_op jit(solution)/shard_map/ppermute | solution.py:42
  64.9 13.1 %all-to-all-start.2 = ((bf16[4,3,16,512]{3,2,1,0:T(8,128)(2,1)}), bf16[4,3,16,512]{3,2,1,0:T(8,128)(2,1)S(1)}, u32[]{:S(2)}, u32[]{:S(2)}) async-start(bf16[4,3,16,512]{3,2,1,0:T(8,128)(2,1)} %shard_map.85), calls=%async_computation.2 | async-start | bytes 393216 | tf_op jit(solution)/shard_map/all_to_all | solution.py:219
  68.3 9.7 %collective-permute-start.3 = (bf16[48,2048]{1,0:T(8,128)(2,1)S(1)}, bf16[48,2048]{1,0:T(8,128)(2,1)S(1)}, u32[]{:S(2)}, u32[]{:S(2)}) collective-permute-start(bf16[48,2048]{1,0:T(8,128)(2,1)S(1)} %get-tuple-element.18), channel_id=1, source_target_pairs={{0,4},{2,6},{4,0},{6,2},{1,5},{3,7},{5,1},{7,3},{8,12},{10,14},{12... | collective-permute-start | bytes 589832 | tf_op jit(solution)/shard_map/ppermute | solution.py:38
  79.3 22.0 %all-to-all-start.3 = ((bf16[8,4,3,16,512]{4,3,2,1,0:T(8,128)(2,1)}), bf16[8,4,3,16,512]{4,3,2,1,0:T(8,128)(2,1)S(1)}, u32[]{:S(2)}, u32[]{:S(2)}) async-start(bf16[8,4,3,16,512]{4,3,2,1,0:T(8,128)(2,1)} %shard_map.87), calls=%async_computation.3 | async-start | bytes 3145728 | tf_op jit(solution)/shard_map/all_to_all | solution.py:223
  83.4 17.9 %copy-start = (bf16[384,512]{1,0:T(8,128)(2,1)S(1)}, bf16[384,512]{1,0:T(8,128)(2,1)}, u32[]{:S(2)}) copy-start(bf16[384,512]{1,0:T(8,128)(2,1)} %q_ref.3) | copy-start | bytes 1179652
  83.4 8.3 %collective-permute-start.4 = (bf16[48,2048]{1,0:T(8,128)(2,1)S(1)}, bf16[48,2048]{1,0:T(8,128)(2,1)S(1)}, u32[]{:S(2)}, u32[]{:S(2)}) collective-permute-start(bf16[48,2048]{1,0:T(8,128)(2,1)S(1)} %get-tuple-element.17), channel_id=1, source_target_pairs={{0,6},{2,4},{4,2},{6,0},{1,7},{3,5},{5,3},{7,1},{8,14},{10,12},{12... | collective-permute-start | bytes 589832 | tf_op jit(solution)/shard_map/ppermute | solution.py:38
  92.7 19.2 %collective-permute-start.5 = (bf16[192,2048]{1,0:T(8,128)(2,1)}, bf16[192,2048]{1,0:T(8,128)(2,1)S(1)}, u32[]{:S(2)}, u32[]{:S(2)}) collective-permute-start(bf16[192,2048]{1,0:T(8,128)(2,1)} %pad_maximum_fusion), channel_id=1, source_target_pairs={{0,1},{1,0},{2,3},{3,2},{4,5},{5,4},{6,7},{7,6},{8,9},{9,8},{10,11... | collective-permute-start | bytes 2359304 | tf_op jit(solution)/shard_map/ppermute | solution.py:42
  102.9 18.8 %all-to-all-start.4 = ((bf16[8,48,512]{2,1,0:T(8,128)(2,1)}), bf16[8,48,512]{2,1,0:T(8,128)(2,1)S(1)}, u32[]{:S(2)}, u32[]{:S(2)}) async-start(bf16[8,48,512]{2,1,0:T(8,128)(2,1)} %shard_map.88), calls=%async_computation.4 | async-start | bytes 786432 | tf_op jit(solution)/shard_map/all_to_all | solution.py:234
  111.9 1.0 copy-start.1

commit v6 on v5

--- a/solution.py
+++ b/solution.py
@@ -205,7 +205,6 @@
     )(fw_key, fw_value, learn_rate.reshape(1, tok_rows), weights)
     pieces = lax.all_to_all(pieces, NEAR, 0, 0, tiled=True)
     before = next_step(kv[0])
-    pieces, before = after(pieces, before)
     pieces = call(sum_body, shape((far, 3, part, width), BF16), (pieces,), 16)
     pieces = lax.all_to_all(pieces, FAR, 0, 0, tiled=True)
     half = call(sum_body, shape((3, part, width), F32), (pieces,), 16)
@@ -214,15 +213,16 @@
     start = lax.dynamic_slice_in_dim(weights, mine, part, 2).transpose(0, 2, 1)
     other = swapped(half, "yh")
     kv += [across(kv[0], before, 1)]
-    other, kv[-1:] = after(other, kv[-1:])
     fresh = call(renorm_body, shape((far, 3, part, width), BF16), (half, other, start), 16)
+    fresh, kv[-1:] = after(fresh, kv[-1:])
     fresh = lax.all_to_all(fresh, FAR, 0, 0, tiled=True)
     kv += [across(kv[0], before, 2)]
     fresh, kv[-1:] = after(fresh, kv[-1:])
     fresh = call(copies_body, shape((close, far, 3, part, width), BF16), (fresh,), 16)
     fresh = lax.all_to_all(fresh, NEAR, 0, 0, tiled=True)
+    early = swapped(jnp.concatenate(kv[:3]), "core")
     kv += [across(kv[0], before, 3)]
-    swap = swapped(jnp.concatenate(kv), "core")
+    fresh, kv, early = (lambda t: (t[0], t[1][0], t[1][1]))(after(fresh, (kv, early)))
 
     fw_out = call(
         answer_body,
@@ -231,6 +231,8 @@
         24,
         3 * product,
     )
+    fw_out, kv = after(fw_out, kv)
+    swap = jnp.concatenate([early, swapped(kv[3], "core")])
     fw_fine = lax.all_to_all(fw_out, HEAD, 0, 0, tiled=True)
     chip, core = lax.axis_index("yl"), lax.axis_index("core")
     heads = lax.axis_size(HEAD)

time: 124 us -> 125 us (level)
  waiting for transfers between devices: 46.6 us -> 55 us
  starting transfers between devices: 58.1 us -> 53.4 us
    all_to_all x1, waiting for transfers between devices: 4.08 us -> 21.3 us  [on_device(): pieces = lax.all_to_all(pieces, NEAR, 0, 0, tiled=True)]
    ppermute x1, waiting for transfers between devices: 17.2 us -> 0.01 us  [next_step(): return lax.ppermute(value, SEQ, [(i, i + 1) for i in range(steps - 1)])]
    all_to_all x1, waiting for transfers between devices: 0.01 us -> 5.63 us  [on_device(): fresh = lax.all_to_all(fresh, NEAR, 0, 0, tiled=True)]
    ppermute x3, waiting for transfers between devices: 10.8 us -> 15.1 us  [across(): return lax.ppermute(block, 'yl', [(i, i ^ away) for i in range(chips)])]
    all_to_all x1, waiting for transfers between devices: 5.2 us -> 2.89 us  [on_device(): fw_fine = lax.all_to_all(fw_out, HEAD, 0, 0, tiled=True)]
    ppermute x2 -> x3, starting transfers between devices: 13.1 us -> 10.9 us  [swapped(): return lax.ppermute(value, axis, [(0, 1), (1, 0)])]
    all_to_all x1, starting transfers between devices: 8.88 us -> 6.78 us  [on_device(): fw_fine = lax.all_to_all(fw_out, HEAD, 0, 0, tiled=True)]
    ppermute x2 -> x3, waiting for transfers between devices: 4.55 us -> 5.48 us  [swapped(): return lax.ppermute(value, axis, [(0, 1), (1, 0)])]
  transfers between devices with their start and end apart: 11 -> 12, of which waited for: 7 -> 8; matrix products, arithmetic and copies ran while one was open for 2% -> 1% of each run, Pallas kernels for 4% -> 4%
where the time goes in v6:
time: 125 us; the launch traced here: 124 us
  waiting for transfers between devices  55 us (44%)
  starting transfers between devices  53.4 us (43%)
  Pallas kernels  14.2 us (11%)
  local copies, waits for them, and re-layouts  1.44 us (1%)
    all_to_all x1, waiting for transfers between devices, on_device(): pieces = lax.all_to_all(pieces, NEAR, 0, 0, tiled=True)  21.3 us
    ppermute x3, waiting for transfers between devices, across(): return lax.ppermute(block, 'yl', [(i, i ^ away) for i in range(chips)])  15.1 us
    ppermute x3, starting transfers between devices, swapped(): return lax.ppermute(value, axis, [(0, 1), (1, 0)])  10.9 us
    ppermute x3, starting transfers between devices, across(): return lax.ppermute(block, 'yl', [(i, i ^ away) for i in range(chips)])  10.2 us
    all_to_all x1, starting transfers between devices, on_device(): pieces = lax.all_to_all(pieces, FAR, 0, 0, tiled=True)  9.12 us
    all_to_all x1, starting transfers between devices, on_device(): fw_fine = lax.all_to_all(fw_out, HEAD, 0, 0, tiled=True)  6.78 us
    all_to_all x1, starting transfers between devices, on_device(): pieces = lax.all_to_all(pieces, NEAR, 0, 0, tiled=True)  5.98 us
    all_to_all x1, waiting for transfers between devices, on_device(): fresh = lax.all_to_all(fresh, NEAR, 0, 0, tiled=True)  5.63 us
  transfers between devices with their start and end apart: 12, of which 8 were waited for; matrix products, arithmetic and copies ran while one was open for 1% of the time, Pallas kernels for 4%

profile of v6, /device:TPU:57, one launch (start us, length us, event | category | flops | bytes accessed | tf_op | source)
XLA Modules:
  0.0 124.5 jit_solution(1813505827962332437)
XLA Ops:
  0.0 5.2 %shard_map.82 = bf16[8,4,3,16,512]{4,3,2,1,0:T(8,128)(2,1)} custom-call(bf16[384,512]{1,0:T(8,128)(2,1)} %k_hbm.1, bf16[384,512]{1,0:T(8,128)(2,1)} %v_hbm.1, f32[1,384]{1,0:T(1,128)} %bitcast.15, bf16[3,512,512]{2,1,0:T(8,128)(2,1)} %bitcast.14), custom_call_target="tpu_custom_call" | custom-call | flops 1207959552 | bytes 4194304 | tf_op jit(solution)/shard_map/pallas_call | solution.py:190
  5.2 0.0 copy-start.2
  5.3 0.0 copy-start.3
  5.3 6.0 %all-to-all-start = ((bf16[8,4,3,16,512]{4,3,2,1,0:T(8,128)(2,1)}), bf16[8,4,3,16,512]{4,3,2,1,0:T(8,128)(2,1)S(1)}, u32[]{:S(2)}, u32[]{:S(2)}) async-start(bf16[8,4,3,16,512]{4,3,2,1,0:T(8,128)(2,1)} %shard_map.82), calls=%async_computation | async-start | bytes 3145728 | tf_op jit(solution)/shard_map/all_to_all | solution.py:206
  11.2 0.0 copy-done.2
  11.3 0.0 copy-done.3
  11.3 3.4 %collective-permute-start.1 = (bf16[48,2048]{1,0:T(8,128)(2,1)S(1)}, bf16[48,2048]{1,0:T(8,128)(2,1)S(1)}, u32[]{:S(2)}, u32[]{:S(2)}) collective-permute-start(bf16[48,2048]{1,0:T(8,128)(2,1)S(1)} %constant_dynamic-update-slice_fusion.refs_0_), channel_id=1, source_target_pairs={{0,8},{8,16},{16,24},{24,32},{32,40},{40,48},{48,56},{56,64},{64,7... | collective-permute-start | bytes 589832 | tf_op jit(solution)/shard_map/ppermute | solution.py:31
  14.7 21.3 %all-to-all-done.in_ref = bf16[8,4,3,16,512]{4,3,2,1,0:T(8,128)(2,1)S(1)} async-done(((bf16[8,4,3,16,512]{4,3,2,1,0:T(8,128)(2,1)}), bf16[8,4,3,16,512]{4,3,2,1,0:T(8,128)(2,1)S(1)}, u32[]{:S(2)}, u32[]{:S(2)}) %all-to-all-start) | async-done | bytes 1572896 | tf_op jit(solution)/shard_map/all_to_all | solution.py:206
  36.0 0.9 shard_map.83
  36.9 9.1 %all-to-all-start.1 = ((bf16[4,3,16,512]{3,2,1,0:T(8,128)(2,1)}), bf16[4,3,16,512]{3,2,1,0:T(8,128)(2,1)S(1)}, u32[]{:S(2)}, u32[]{:S(2)}) async-start(bf16[4,3,16,512]{3,2,1,0:T(8,128)(2,1)} %shard_map.83), calls=%async_computation.1 | async-start | bytes 393216 | tf_op jit(solution)/shard_map/all_to_all | solution.py:209
  46.0 0.0 collective-permute-done.1
  46.0 3.0 %collective-permute-start.2 = (bf16[48,2048]{1,0:T(8,128)(2,1)S(1)}, bf16[48,2048]{1,0:T(8,128)(2,1)S(1)}, u32[]{:S(2)}, u32[]{:S(2)}) collective-permute-start(bf16[48,2048]{1,0:T(8,128)(2,1)S(1)} %get-tuple-element.37), channel_id=1, source_target_pairs={{0,2},{2,0},{4,6},{6,4},{1,3},{3,1},{5,7},{7,5},{8,10},{10,8},{12,... | collective-permute-start | bytes 589832 | tf_op jit(solution)/shard_map/ppermute | solution.py:38
  49.0 4.6 %all-to-all-done.1.in_ref = bf16[4,3,16,512]{3,2,1,0:T(8,128)(2,1)S(1)} async-done(((bf16[4,3,16,512]{3,2,1,0:T(8,128)(2,1)}), bf16[4,3,16,512]{3,2,1,0:T(8,128)(2,1)S(1)}, u32[]{:S(2)}, u32[]{:S(2)}) %all-to-all-start.1) | async-done | bytes 196640 | tf_op jit(solution)/shard_map/all_to_all | solution.py:209
  53.7 4.4 %collective-permute-start = (f32[3,16,512]{2,1,0:T(8,128)S(1)}, f32[3,16,512]{2,1,0:T(8,128)S(1)}, u32[]{:S(2)}, u32[]{:S(2)}) collective-permute-start(f32[3,16,512]{2,1,0:T(8,128)S(1)} %shard_map.84.half_ref), channel_id=1, source_target_pairs={{0,256},{256,0},{1,257},{257,1},{2,258},{258,2},{3,259},{259,3},{4... | collective-permute-start | bytes 294920 | tf_op jit(solution)/shard_map/ppermute | solution.py:42
  58.1 1.2 constant_dynamic-slice_fusion
  59.3 0.1 copy.9
  59.5 4.5 %collective-permute-done.other_ref = f32[3,16,512]{2,1,0:T(8,128)S(1)} collective-permute-done((f32[3,16,512]{2,1,0:T(8,128)S(1)}, f32[3,16,512]{2,1,0:T(8,128)S(1)}, u32[]{:S(2)}, u32[]{:S(2)}) %collective-permute-start) | collective-permute-done | bytes 98336 | tf_op jit(solution)/shard_map/ppermute | solution.py:42
  64.0 0.8 shard_map.85
  64.8 0.0 collective-permute-done.2.refs_1_
  64.8 3.4 %all-to-all-start.2 = ((bf16[4,3,16,512]{3,2,1,0:T(8,128)(2,1)}), bf16[4,3,16,512]{3,2,1,0:T(8,128)(2,1)S(1)}, u32[]{:S(2)}, u32[]{:S(2)}) async-start(bf16[4,3,16,512]{3,2,1,0:T(8,128)(2,1)} %shard_map.85), calls=%async_computation.2 | async-start | bytes 393216 | tf_op jit(solution)/shard_map/all_to_all | solution.py:218
  68.2 3.1 %collective-permute-start.3 = (bf16[48,2048]{1,0:T(8,128)(2,1)S(1)}, bf16[48,2048]{1,0:T(8,128)(2,1)S(1)}, u32[]{:S(2)}, u32[]{:S(2)}) collective-permute-start(bf16[48,2048]{1,0:T(8,128)(2,1)S(1)} %get-tuple-element.36), channel_id=1, source_target_pairs={{0,4},{2,6},{4,0},{6,2},{1,5},{3,7},{5,1},{7,3},{8,12},{10,14},{12... | collective-permute-start | bytes 589832 | tf_op jit(solution)/shard_map/ppermute | solution.py:38
  71.3 8.9 %collective-permute-done.3.refs_2_ = bf16[48,2048]{1,0:T(8,128)(2,1)S(1)} collective-permute-done((bf16[48,2048]{1,0:T(8,128)(2,1)S(1)}, bf16[48,2048]{1,0:T(8,128)(2,1)S(1)}, u32[]{:S(2)}, u32[]{:S(2)}) %collective-permute-start.3) | collective-permute-done | bytes 196640 | tf_op jit(solution)/shard_map/ppermute | solution.py:38
  80.2 0.0 all-to-all-done.2.in_ref
  80.2 1.3 %shard_map.86 = bf16[8,4,3,16,512]{4,3,2,1,0:T(8,128)(2,1)} custom-call(bf16[4,3,16,512]{3,2,1,0:T(8,128)(2,1)S(1)} %all-to-all-done.2.in_ref), custom_call_target="tpu_custom_call" | custom-call | bytes 1769472 | tf_op jit(solution)/shard_map/pallas_call | solution.py:51
  81.5 0.0 copy-start
  81.5 3.7 %all-to-all-start.3 = ((bf16[8,4,3,16,512]{4,3,2,1,0:T(8,128)(2,1)}), bf16[8,4,3,16,512]{4,3,2,1,0:T(8,128)(2,1)S(1)}, u32[]{:S(2)}, u32[]{:S(2)}) async-start(bf16[8,4,3,16,512]{4,3,2,1,0:T(8,128)(2,1)} %shard_map.86), calls=%async_computation.3 | async-start | bytes 3145728 | tf_op jit(solution)/shard_map/all_to_all | solution.py:222
  85.3 4.2 %collective-permute-start.5 = (bf16[144,2048]{1,0:T(8,128)(2,1)S(1)}, bf16[144,2048]{1,0:T(8,128)(2,1)S(1)}, u32[]{:S(2)}, u32[]{:S(2)}) collective-permute-start(bf16[144,2048]{1,0:T(8,128)(2,1)S(1)} %pad_maximum_fusion.1), channel_id=1, source_target_pairs={{0,1},{1,0},{2,3},{3,2},{4,5},{5,4},{6,7},{7,6},{8,9},{9,8},{10,11... | collective-permute-start | bytes 1769480 | tf_op jit(solution)/shard_map/ppermute | solution.py:42
  89.5 4.0 %collective-permute-start.4 = (bf16[48,2048]{1,0:T(8,128)(2,1)S(1)}, bf16[48,2048]{1,0:T(8,128)(2,1)S(1)}, u32[]{:S(2)}, u32[]{:S(2)}) collective-permute-start(bf16[48,2048]{1,0:T(8,128)(2,1)S(1)} %get-tuple-element.35), channel_id=1, source_target_pairs={{0,6},{2,4},{4,2},{6,0},{1,7},{3,5},{5,3},{7,1},{8,14},{10,12},{12... | collective-permute-start | bytes 589832 | tf_op jit(solution)/shard_map/ppermute | solution.py:38
  93.5 6.2 %collective-permute-done.4.refs_3_ = bf16[48,2048]{1,0:T(8,128)(2,1)S(1)} collective-permute-done((bf16[48,2048]{1,0:T(8,128)(2,1)S(1)}, bf16[48,2048]{1,0:T(8,128)(2,1)S(1)}, u32[]{:S(2)}, u32[]{:S(2)}) %collective-permute-start.4) | collective-permute-done | bytes 196640 | tf_op jit(solution)/shard_map/ppermute | solution.py:38
  99.7 0.0 collective-permute-done.5
  99.7 5.6 %all-to-all-done.3.w_ref = bf16[8,4,3,16,512]{4,3,2,1,0:T(8,128)(2,1)S(1)} async-done(((bf16[8,4,3,16,512]{4,3,2,1,0:T(8,128)(2,1)}), bf16[8,4,3,16,512]{4,3,2,1,0:T(8,128)(2,1)S(1)}, u32[]{:S(2)}, u32[]{:S(2)}) %all-to-all-start.3) | async-done | bytes 1572896 | tf_op jit(solution)/shard_map/all_to_all | solution.py:222
  105.4 0.0 copy-done
  105.4 1.6 %shard_map.87 = bf16[8,48,512]{2,1,0:T(8,128)(2,1)} custom-call(bf16[384,512]{1,0:T(8,128)(2,1)S(1)} %copy-done, bf16[8,4,3,16,512]{4,3,2,1,0:T(8,128)(2,1)S(1)} %all-to-all-done.3.w_ref), custom_call_target="tpu_custom_call" | custom-call | flops 603979776 | bytes 2359296 | tf_op jit(solution)/shard_map/pallas_call | solution.py:51
  107.0 0.0 copy-start.1
  107.0 6.8 %all-to-all-start.4 = ((bf16[8,48,512]{2,1,0:T(8,128)(2,1)}), bf16[8,48,512]{2,1,0:T(8,128)(2,1)S(1)}, u32[]{:S(2)}, u32[]{:S(2)}) async-start(bf16[8,48,512]{2,1,0:T(8,128)(2,1)} %shard_map.87), calls=%async_computation.4 | async-start | bytes 786432 | tf_op jit(solution)/shard_map/all_to_all | solution.py:236
  113.8 2.3 %collective-permute-start.6 = (bf16[48,2048]{1,0:T(8,128)(2,1)S(1)}, bf16[48,2048]{1,0:T(8,128)(2,1)S(1)}, u32[]{:S(2)}, u32[]{:S(2)}) collective-permute-start(bf16[48,2048]{1,0:T(8,128)(2,1)S(1)} %collective-permute-done.4.refs_3_), channel_id=1, source_target_pairs={{0,1},{1,0},{2,3},{3,2},{4,5},{5,4},{6,7},{7,6},{8,9},{9,8},{10,11... | collective-permute-start | bytes 589832 | tf_op jit(solution)/shard_map/ppermute | solution.py:42
  116.1 0.1 stack.35.place_ref
  116.2 0.9 collective-permute-done.6
  117.1 0.1 pad_maximum_fusion.refs_4_
  117.1 0.0 copy-done.1
  117.2 3.6 %shard_map.88.attn_ref = f32[48,4096]{1,0:T(8,128)S(1)} custom-call(s32[8]{0:T(128)S(1)} %stack.35.place_ref, bf16[48,4096]{1,0:T(8,128)(2,1)S(1)} %copy-done.1, bf16[48,2048]{1,0:T(8,128)(2,1)S(1)} %constant_dynamic-update-slice_fusion.refs_0_, bf16[48,2048]{1,0:T(8,128)(2,1)S(1)} %collective-permute-done.2.refs_1_, ...), custom_call_target="tpu_custom_call" | custom-call | flops 1000000000 | bytes 3145728 | tf_op jit(solution)/shard_map/pallas_call | solution.py:248
  120.7 2.9 %all-to-all-done.4.fw_ref = bf16[8,48,512]{2,1,0:T(8,128)(2,1)S(1)} async-done(((bf16[8,48,512]{2,1,0:T(8,128)(2,1)}), bf16[8,48,512]{2,1,0:T(8,128)(2,1)S(1)}, u32[]{:S(2)}, u32[]{:S(2)}) %all-to-all-start.4) | async-done | bytes 393248 | tf_op jit(solution)/shard_map/all_to_all | solution.py:236
  123.6 0.8 shard_map.89
  (5 shorter events, 0.1 us)
Async XLA Ops:
  5.2 6.0 %copy-start.2 = (bf16[48,1024]{1,0:T(8,128)(2,1)S(1)}, bf16[48,1024]{1,0:T(8,128)(2,1)}, u32[]{:S(2)}) copy-start(bf16[48,1024]{1,0:T(8,128)(2,1)} %param.14) | copy-start | bytes 294916
  5.3 6.0 %copy-start.3 = (bf16[48,1024]{1,0:T(8,128)(2,1)S(1)}, bf16[48,1024]{1,0:T(8,128)(2,1)}, u32[]{:S(2)}) copy-start(bf16[48,1024]{1,0:T(8,128)(2,1)} %param.15) | copy-start | bytes 294916
  5.3 30.7 %all-to-all-start = ((bf16[8,4,3,16,512]{4,3,2,1,0:T(8,128)(2,1)}), bf16[8,4,3,16,512]{4,3,2,1,0:T(8,128)(2,1)S(1)}, u32[]{:S(2)}, u32[]{:S(2)}) async-start(bf16[8,4,3,16,512]{4,3,2,1,0:T(8,128)(2,1)} %shard_map.82), calls=%async_computation | async-start | bytes 3145728 | tf_op jit(solution)/shard_map/all_to_all | solution.py:206
  11.3 34.7 %collective-permute-start.1 = (bf16[48,2048]{1,0:T(8,128)(2,1)S(1)}, bf16[48,2048]{1,0:T(8,128)(2,1)S(1)}, u32[]{:S(2)}, u32[]{:S(2)}) collective-permute-start(bf16[48,2048]{1,0:T(8,128)(2,1)S(1)} %constant_dynamic-update-slice_fusion.refs_0_), channel_id=1, source_target_pairs={{0,8},{8,16},{16,24},{24,32},{32,40},{40,48},{48,56},{56,64},{64,7... | collective-permute-start | bytes 589832 | tf_op jit(solution)/shard_map/ppermute | solution.py:31
  36.9 16.8 %all-to-all-start.1 = ((bf16[4,3,16,512]{3,2,1,0:T(8,128)(2,1)}), bf16[4,3,16,512]{3,2,1,0:T(8,128)(2,1)S(1)}, u32[]{:S(2)}, u32[]{:S(2)}) async-start(bf16[4,3,16,512]{3,2,1,0:T(8,128)(2,1)} %shard_map.83), calls=%async_computation.1 | async-start | bytes 393216 | tf_op jit(solution)/shard_map/all_to_all | solution.py:209
  46.0 18.8 %collective-permute-start.2 = (bf16[48,2048]{1,0:T(8,128)(2,1)S(1)}, bf16[48,2048]{1,0:T(8,128)(2,1)S(1)}, u32[]{:S(2)}, u32[]{:S(2)}) collective-permute-start(bf16[48,2048]{1,0:T(8,128)(2,1)S(1)} %get-tuple-element.37), channel_id=1, source_target_pairs={{0,2},{2,0},{4,6},{6,4},{1,3},{3,1},{5,7},{7,5},{8,10},{10,8},{12,... | collective-permute-start | bytes 589832 | tf_op jit(solution)/shard_map/ppermute | solution.py:38
  53.7 10.3 %collective-permute-start = (f32[3,16,512]{2,1,0:T(8,128)S(1)}, f32[3,16,512]{2,1,0:T(8,128)S(1)}, u32[]{:S(2)}, u32[]{:S(2)}) collective-permute-start(f32[3,16,512]{2,1,0:T(8,128)S(1)} %shard_map.84.half_ref), channel_id=1, source_target_pairs={{0,256},{256,0},{1,257},{257,1},{2,258},{258,2},{3,259},{259,3},{4... | collective-permute-start | bytes 294920 | tf_op jit(solution)/shard_map/ppermute | solution.py:42
  64.8 15.4 %all-to-all-start.2 = ((bf16[4,3,16,512]{3,2,1,0:T(8,128)(2,1)}), bf16[4,3,16,512]{3,2,1,0:T(8,128)(2,1)S(1)}, u32[]{:S(2)}, u32[]{:S(2)}) async-start(bf16[4,3,16,512]{3,2,1,0:T(8,128)(2,1)} %shard_map.85), calls=%async_computation.2 | async-start | bytes 393216 | tf_op jit(solution)/shard_map/all_to_all | solution.py:218
  68.2 12.0 %collective-permute-start.3 = (bf16[48,2048]{1,0:T(8,128)(2,1)S(1)}, bf16[48,2048]{1,0:T(8,128)(2,1)S(1)}, u32[]{:S(2)}, u32[]{:S(2)}) collective-permute-start(bf16[48,2048]{1,0:T(8,128)(2,1)S(1)} %get-tuple-element.36), channel_id=1, source_target_pairs={{0,4},{2,6},{4,0},{6,2},{1,5},{3,7},{5,1},{7,3},{8,12},{10,14},{12... | collective-permute-start | bytes 589832 | tf_op jit(solution)/shard_map/ppermute | solution.py:38
  81.5 23.9 %copy-start = (bf16[384,512]{1,0:T(8,128)(2,1)S(1)}, bf16[384,512]{1,0:T(8,128)(2,1)}, u32[]{:S(2)}) copy-start(bf16[384,512]{1,0:T(8,128)(2,1)} %q_ref.2) | copy-start | bytes 1179652
  81.5 23.9 %all-to-all-start.3 = ((bf16[8,4,3,16,512]{4,3,2,1,0:T(8,128)(2,1)}), bf16[8,4,3,16,512]{4,3,2,1,0:T(8,128)(2,1)S(1)}, u32[]{:S(2)}, u32[]{:S(2)}) async-start(bf16[8,4,3,16,512]{4,3,2,1,0:T(8,128)(2,1)} %shard_map.86), calls=%async_computation.3 | async-start | bytes 3145728 | tf_op jit(solution)/shard_map/all_to_all | solution.py:222
  85.3 14.5 %collective-permute-start.5 = (bf16[144,2048]{1,0:T(8,128)(2,1)S(1)}, bf16[144,2048]{1,0:T(8,128)(2,1)S(1)}, u32[]{:S(2)}, u32[]{:S(2)}) collective-permute-start(bf16[144,2048]{1,0:T(8,128)(2,1)S(1)} %pad_maximum_fusion.1), channel_id=1, source_target_pairs={{0,1},{1,0},{2,3},{3,2},{4,5},{5,4},{6,7},{7,6},{8,9},{9,8},{10,11... | collective-permute-start | bytes 1769480 | tf_op jit(solution)/shard_map/ppermute | solution.py:42
  89.5 10.3 %collective-permute-start.4 = (bf16[48,2048]{1,0:T(8,128)(2,1)S(1)}, bf16[48,2048]{1,0:T(8,128)(2,1)S(1)}, u32[]{:S(2)}, u32[]{:S(2)}) collective-permute-start(bf16[48,2048]{1,0:T(8,128)(2,1)S(1)} %get-tuple-element.35), channel_id=1, source_target_pairs={{0,6},{2,4},{4,2},{6,0},{1,7},{3,5},{5,3},{7,1},{8,14},{10,12},{12... | collective-permute-start | bytes 589832 | tf_op jit(solution)/shard_map/ppermute | solution.py:38
  107.0 10.2 %copy-start.1 = (bf16[48,4096]{1,0:T(8,128)(2,1)S(1)}, bf16[48,4096]{1,0:T(8,128)(2,1)}, u32[]{:S(2)}) copy-start(bf16[48,4096]{1,0:T(8,128)(2,1)} %q_ref.3) | copy-start | bytes 1179652
  107.0 16.7 %all-to-all-start.4 = ((bf16[8,48,512]{2,1,0:T(8,128)(2,1)}), bf16[8,48,512]{2,1,0:T(8,128)(2,1)S(1)}, u32[]{:S(2)}, u32[]{:S(2)}) async-start(bf16[8,48,512]{2,1,0:T(8,128)(2,1)} %shard_map.87), calls=%async_computation.4 | async-start | bytes 786432 | tf_op jit(solution)/shard_map/all_to_all | solution.py:236
  113.8 3.3 %collective-permute-start.6 = (bf16[48,2048]{1,0:T(8,128)(2,1)S(1)}, bf16[48,2048]{1,0:T(8,128)(2,1)S(1)}, u32[]{:S(2)}, u32[]{:S(2)}) collective-permute-start(bf16[48,2048]{1,0:T(8,128)(2,1)S(1)} %collective-permute-done.4.refs_3_), channel_id=1, source_target_pairs={{0,1},{1,0},{2,3},{3,2},{4,5},{5,4},{6,7},{7,6},{8,9},{9,8},{10,11... | collective-permute-start | bytes 589832 | tf_op jit(solution)/shard_map/ppermute | solution.py:42
